TPU v7x, 128 devices: a whole 4x4x4 slice. The times are simulated.
128 devices in a mesh: tm: 32 (over z, x, core), height: 4 (over y).
Axes of the slice: x: 4, y: 4, z: 4, core: 2. Of those that a mesh axis runs over, the one named last changes fastest.
Arguments:
- video: bfloat16 [128, 32, 160, 128], P('tm', 'height'), as said below
- conv_weight: bfloat16 [3, 3, 3, 128, 128], replicated, may hold values from -0.109375 to 0.109375
- norm_gain: float32 [128], replicated, may hold values from 0.25 to 1.75
- norm_bias: float32 [128], replicated, may hold values from -3 to 3
- down_weight: bfloat16 [512, 256], replicated, may hold values from -0.25 to 0.25
- length_table: float32 [8, 256], replicated, may hold values from -3 to 3
- keep: int32 [128, 16, 80], P('tm', 'height'), may hold values from 0 to 1, as said below
- run_length: int32 [128, 16, 80], P('tm', 'height'), may hold values from 1 to 8
- owner: int32 [128, 16, 80], P('tm', 'height'), may hold values from 0 to 127
Outputs:
- latent: bfloat16 [128, 16, 80, 256], P('tm', 'height')
- routed: bfloat16 [131072, 256], P(('tm', 'height'))
Inputs may be any that keep to these rules, and one draw needn't show every extreme that they name: `keep`: kept patches of one block (the patches of one device) going to one owner number at most 8; in every draw some owner receives exactly 8 from every block. Such per-owner counts may cross devices packed several to a word. `video`: values within -40 to 40.
All inputs are finite; a program needn't handle non-finite values.
Results may differ from a plain program's by a relative error of at most 0.0052.
Values may be sent and summed in bfloat16 or wider, within the bound.
A program may use at most 128 MiB of HBM per device.

v0:
```python
import jax
import jax.numpy as jnp
from jax import lax
from jax.sharding import PartitionSpec as P

GROUPS = 32
LMAX = 8
CAP = 8


EPSILON = 1e-06


def passed_along(block, axis, distance):
    devices = range(lax.axis_size(axis))
    route = [(i - distance, i) for i in devices if i - distance in devices]
    return lax.ppermute(block, axis, route)


def padded_2(cells, sides, width):
    for axis, dim in sides:
        count = lax.axis_size(axis)
        ends = count - 1
        head = lax.slice_in_dim(cells, 0, width, axis=dim)
        tail = lax.slice_in_dim(cells, cells.shape[dim] - width, cells.shape[dim], axis=dim)
        cells = jnp.concatenate(
            [
                lax.ppermute(tail, axis, [(i, (i + 1) % count) for i in range(ends)]),
                cells,
                lax.ppermute(head, axis, [((i + 1) % count, i) for i in range(ends)]),
            ],
            axis=dim,
        )
    return cells


def carried_in(array, axis, combine, identity):
    count, here = (lax.axis_size(axis), lax.axis_index(axis))
    everything = lax.all_gather(array, axis)
    start = jnp.broadcast_to(jnp.asarray(identity, array.dtype), array.shape)

    def turn(k, before):
        reached = k < here
        new = combine(before, everything[k])
        return jnp.where(reached, new, before)

    return lax.fori_loop(0, count, turn, start)


def add_counts(earlier, later):
    return earlier + later


def deliver(outgoing, sent_ints, owners, width_out):
    arrived, arrived_ints = (
        lax.all_to_all(
            outgoing.reshape(owners, CAP, width_out),
            ("tm", "height"),
            split_axis=0,
            concat_axis=0,
            tiled=True,
        ),
        lax.all_to_all(
            sent_ints.reshape(owners, 1), ("tm", "height"), split_axis=0, concat_axis=0, tiled=True
        ),
    )
    return (arrived, arrived_ints.reshape(owners))


def on_device(
    video, conv_weight, norm_gain, norm_bias, down_weight, length_table, keep, run_length, owner
):
    frames, rows, columns, channels = video.shape
    width_out = down_weight.shape[1]
    earlier = passed_along(video[frames - 2 :], "tm", 1)
    stacked = jnp.concatenate([earlier, video], axis=0)
    rimmed = padded_2(stacked, (("height", 1),), 1)
    padded = jnp.pad(rimmed, ((0, 0), (0, 0), (1, 1), (0, 0)))
    widened = jnp.concatenate(
        [padded[:, :, 0:columns], padded[:, :, 1 : columns + 1], padded[:, :, 2 : columns + 2]],
        axis=3,
    )
    folded = conv_weight.reshape(3, 3, 3 * channels, channels)
    hidden = jnp.zeros((frames * rows * columns, channels), jnp.float32)
    for frame_tap in range(3):
        for row_tap in range(3):
            window = widened[frame_tap : frame_tap + frames, row_tap : row_tap + rows].reshape(
                -1, 3 * channels
            )
            hidden = hidden + jnp.dot(
                window, folded[frame_tap, row_tap], preferred_element_type=jnp.float32
            )
    group_width = channels // GROUPS
    grouped = hidden.reshape(frames, rows * columns, GROUPS, group_width)
    totals = jnp.sum(grouped, axis=(1, 3))
    squared = jnp.sum(grouped * grouped, axis=(1, 3))
    totals, squared = lax.psum((totals, squared), "height")
    count = rows * lax.axis_size("height") * columns * group_width
    average = totals / count
    squares = squared / count
    spread = squares - average * average
    normed = (grouped - average[:, None, :, None]) * lax.rsqrt(spread + EPSILON)[:, None, :, None]
    normed = normed.reshape(frames, rows, columns, channels) * norm_gain + norm_bias
    active = jax.nn.silu(normed).astype(jnp.bfloat16)
    half_rows = rows // 2
    half_columns = columns // 2
    patched = (
        active.reshape(frames, half_rows, 2, half_columns, 2, channels)
        .transpose(0, 1, 3, 2, 4, 5)
        .reshape(-1, 4 * channels)
    )
    latent = jnp.dot(patched, down_weight, preferred_element_type=jnp.float32).astype(jnp.bfloat16)
    owners = lax.axis_size("tm") * lax.axis_size("height")
    flat_keep = keep.reshape(-1)
    flat_owner = owner.reshape(-1)
    flat_run = run_length.reshape(-1)
    lookup = (flat_run[:, None] - 1 == jnp.arange(LMAX, dtype=jnp.int32)[None, :]).astype(
        jnp.float32
    )
    extra = jnp.dot(lookup, length_table, precision=lax.Precision.HIGHEST)
    values = (latent.astype(jnp.float32) + extra).astype(jnp.bfloat16)
    member = (
        (flat_owner[:, None] == jnp.arange(owners, dtype=jnp.int32)[None, :])
        & (flat_keep[:, None] == 1)
    ).astype(jnp.int32)
    counts = jnp.sum(member, axis=0)
    before = jnp.cumsum(member, axis=0) - member
    rank = jnp.sum(before * member, axis=1)
    slot = jnp.where(flat_keep == 1, flat_owner * CAP + rank, owners * CAP)
    outgoing = jnp.zeros((owners * CAP, width_out), jnp.bfloat16).at[slot].set(values, mode="drop")
    sent_ints = carried_in(counts, ("tm", "height"), add_counts, jnp.zeros_like(counts))
    arrived, arrived_ints = deliver(outgoing, sent_ints, owners, width_out)
    spots = (arrived_ints[:, None] + jnp.arange(CAP, dtype=jnp.int32)[None, :]).reshape(-1)
    routed = (
        jnp.zeros((owners * CAP, width_out), jnp.bfloat16)
        .at[spots]
        .add(arrived.reshape(-1, width_out), mode="drop")
    )
    return (latent.reshape(frames, half_rows, half_columns, width_out), routed)


def solution(mesh):
    return jax.shard_map(
        on_device,
        mesh=mesh,
        in_specs=(
            P("tm", "height", None, None),
            P(),
            P(),
            P(),
            P(),
            P(),
            P("tm", "height", None),
            P("tm", "height", None),
            P("tm", "height", None),
        ),
        out_specs=(P("tm", "height", None, None), P(("tm", "height"), None)),
        check_vma=False,
    )
```

profile of v0, /device:TPU:1, one launch (start us, length us, event | category | flops | bytes accessed | tf_op | source)
XLA Modules:
  0.0 200.0 jit_solution(16495996543598376625)
XLA Ops:
  1.8 4.5 %collective-permute-start = (bf16[2,8,160,128]{3,2,1,0:T(8,128)(2,1)S(1)}, bf16[2,8,160,128]{3,2,1,0:T(8,128)(2,1)}, u32[]{:S(2)}, u32[]{:S(2)}) collective-permute-start(bf16[2,8,160,128]{3,2,1,0:T(8,128)(2,1)S(1)} %slice.76), channel_id=1, source_target_pairs={{0,4},{4,8},{8,12},{12,16},{16,20},{20,24},{24,28},{28,32},{32,36}... | collective-permute-start | bytes 1966088 | tf_op jit(solution)/shard_map/ppermute | solution.py:17
  11.1 46.4 %all-gather.1 = s32[128,1,128]{2,1,0:T(1,128)S(1)} all-gather(s32[1,1,128]{2,1,0:T(1,128)S(1)} %bitcast.98), channel_id=2, replica_groups=mesh['tm'=32,'height'=4] {'tm','height'}, dimensions={0}, use_global_device_ids=true | all-gather | bytes 66048 | tf_op jit(solution)/shard_map/all_gather | solution.py:39
  57.5 5.2 %while.14 = (s32[]{:T(128)}, s32[128]{0:T(128)S(1)}, s32[]{:T(128)}, s32[128,128]{1,0:T(8,128)S(1)}, s32[]{:T(128)}, /*index=5*/s32[]{:T(128)}) while((s32[]{:T(128)}, s32[128]{0:T(128)S(1)}, s32[]{:T(128)}, s32[128,128]{1,0:T(8,128)S(1)}, s32[]{:T(128)}, /*index=5*/s32[]{:T(128)}) %tuple.52), condition=%wide.region_6.7_spmd.clone, body=%wide.region_5.6_spmd.clone.sunk | while | flops 388 | bytes 1629 | solution.py:47
  63.4 6.8 %all-to-all-start = ((s32[128,1,1]{2,1,0:T(1,128)}), s32[128,1,1]{2,1,0:T(1,128)}, u32[]{:S(2)}, u32[]{:S(2)}) async-start(s32[128,1,1]{2,1,0:T(1,128)} %copy.47), calls=%async_computation | async-start | bytes 131072 | tf_op jit(solution)/shard_map/all_to_all | solution.py:63
  73.0 3.3 %collective-permute-start.1 = (bf16[6,1,160,128]{3,2,1,0:T(8,128)(2,1)S(1)}, bf16[6,1,160,128]{3,2,1,0:T(8,128)(2,1)S(1)}, u32[]{:S(2)}, u32[]{:S(2)}) collective-permute-start(bf16[6,1,160,128]{3,2,1,0:T(8,128)(2,1)S(1)} %get-tuple-element.122), channel_id=1, source_target_pairs={{0,1},{1,2},{2,3},{4,5},{5,6},{6,7},{8,9},{9,10},{10,11},{12,13},{... | collective-permute-start | bytes 737288 | tf_op jit(solution)/shard_map/ppermute | solution.py:28
  76.3 1.3 collective-permute-start.2
  78.4 2.8 %collective-permute-done.1 = bf16[6,1,160,128]{3,2,1,0:T(8,128)(2,1)S(1)} collective-permute-done((bf16[6,1,160,128]{3,2,1,0:T(8,128)(2,1)S(1)}, bf16[6,1,160,128]{3,2,1,0:T(8,128)(2,1)S(1)}, u32[]{:S(2)}, u32[]{:S(2)}) %collective-permute-start.1) | collective-permute-done | bytes 245792 | tf_op jit(solution)/shard_map/ppermute | solution.py:28
  81.2 3.8 %collective-permute-done.2 = bf16[6,1,160,128]{3,2,1,0:T(8,128)(2,1)S(1)} collective-permute-done((bf16[6,1,160,128]{3,2,1,0:T(8,128)(2,1)S(1)}, bf16[6,1,160,128]{3,2,1,0:T(8,128)(2,1)S(1)}, u32[]{:S(2)}, u32[]{:S(2)}) %collective-permute-start.2) | collective-permute-done | bytes 245792 | tf_op jit(solution)/shard_map/ppermute | solution.py:30
  86.1 1.6 fusion.44
  87.7 3.8 %pad_maximum_fusion = bf16[6,10,160,384]{3,2,1,0:T(8,128)(2,1)} fusion(bf16[6,10,160,128]{3,2,1,0:T(8,128)(2,1)S(1)} %get-tuple-element.121, bf16[6,1,160,128]{3,2,1,0:T(8,128)(2,1)S(1)} %collective-permute-done.2, bf16[6,8,160,128]{3,2,1,0:T(8,128)(2,1)S(1)} %constant_dynamic-update-slice_fusion, bf16[6,1,160,128]{3,2,1,0:T(8,128)(2,1)S(1)} %collective-permute-done.1, ...), kind=kLoop, calls=%fused_computation.6 | loop fusion | flops 36864000 | bytes 14745600 | tf_op jit(solution)/shard_map/concatenate | solution.py:79
  91.5 24.0 %fusion.43 = (bf16[4,8,160,384]{3,2,1,0:T(8,128)(2,1)}, bf16[4,8,160,384]{3,2,1,0:T(8,128)(2,1)}, bf16[4,8,160,384]{3,2,1,0:T(8,128)(2,1)}, bf16[4,8,160,384]{3,...) fusion(bf16[6,10,160,384]{3,2,1,0:T(8,128)(2,1)} %pad_maximum_f, ...), kind=kLoop, calls=%fused_computation.81 | loop fusion | bytes 70778880 | tf_op jit(solution)/shard_map/slice | solution.py:87
  115.5 3.4 %fusion.33 = f32[5120,128]{1,0:T(8,128)S(1)} fusion(bf16[5120,384]{1,0:T(8,128)(2,1)} %bitcast.82, bf16[3,3,384,128]{3,2,1,0:T(8,128)(2,1)S(1)} %bitcast.86), kind=kOutput, calls=%fused_computation.52 | convolution fusion | flops 503316480 | bytes 6651904 | tf_op jit(solution)/shard_map/dot_general | solution.py:90
  129.6 2.7 %fusion.39 = f32[5120,128]{1,0:T(8,128)} fusion(bf16[5120,384]{1,0:T(8,128)(2,1)S(1)} %bitcast.76, bf16[3,3,384,128]{3,2,1,0:T(8,128)(2,1)S(1)} %bitcast.92), kind=kOutput, calls=%fused_computation.64 | convolution fusion | flops 503316480 | bytes 6651904 | tf_op jit(solution)/shard_map/dot_general | solution.py:90
  132.3 2.7 %fusion.40 = f32[5120,128]{1,0:T(8,128)} fusion(bf16[5120,384]{1,0:T(8,128)(2,1)S(1)} %bitcast.75, bf16[3,3,384,128]{3,2,1,0:T(8,128)(2,1)S(1)} %bitcast.93), kind=kOutput, calls=%fused_computation.66 | convolution fusion | flops 503316480 | bytes 6651904 | tf_op jit(solution)/shard_map/dot_general | solution.py:90
  135.0 4.2 %fusion.6 = f32[5120,128]{1,0:T(8,128)S(1)} fusion(f32[5120,128]{1,0:T(8,128)S(1)} %fusion.33, f32[5120,128]{1,0:T(8,128)S(1)} %fusion.34, f32[5120,128]{1,0:T(8,128)S(1)} %fusion.35, f32[5120,128]{1,0:T(8,128)S(1)} %fusion.36, f32[5120,128]{1,0:T(8,128)S(1)} %fusion.37, f32[5120,128]{1,0:T(8,128)S(1)} %fusion.38, f32[5120,128]{1,0:T(8,128)} %fusion.39, ...), kind=kOutput, calls=%fused_computation.14 | convolution fusion | flops 508559360 | bytes 27623424 | tf_op jit(solution)/shard_map/dot_general | solution.py:90
  139.2 2.1 %copy.42 = f32[5120,128]{0,1:T(8,128)} copy(f32[5120,128]{1,0:T(8,128)S(1)} %fusion.6) | data formatting | bytes 5242880 | tf_op jit(solution)/shard_map/add | solution.py:90
  141.3 4.0 %reshape.193 = f32[4,1280,32,4]{1,0,3,2:T(4,128)} reshape(f32[5120,128]{0,1:T(8,128)} %copy.42) | data formatting | bytes 5242880 | tf_op jit(solution)/shard_map/reshape | solution.py:94
  145.3 2.8 %fusion.42 = (f32[4,32]{0,1:T(8,128)S(1)}, f32[4,32]{0,1:T(8,128)S(1)}) fusion(f32[4,1280,32,4]{1,0,3,2:T(4,128)} %reshape.193), kind=kLoop, calls=%fused_computation.80 | loop fusion | flops 1965824 | bytes 2622464 | tf_op jit(solution)/shard_map/reduce_sum | solution.py:95
  148.2 7.5 %all-reduce.1 = (f32[4,32]{1,0:T(4,128)S(1)}, f32[4,32]{1,0:T(4,128)S(1)}) all-reduce(f32[4,32]{1,0:T(4,128)S(1)} %copy.45, f32[4,32]{1,0:T(4,128)S(1)} %copy.43), channel_id=1, replica_groups=mesh['tm'=32,'height'=4] {'height'}, use_global_device_ids=true, to_apply=%region_3.4 | all-reduce | flops 256 | bytes 2048 | tf_op jit(solution)/shard_map/psum | solution.py:97
  160.0 8.7 %scatter_custom_fusion = bf16[1024,256]{1,0:T(8,128)(2,1)} fusion(s32[1280]{0:T(1024)S(1)} %fusion.41, bf16[1280,256]{1,0:T(8,128)(2,1)S(1)} %fusion.14, bf16[]{:T(256)} %constant.53.clone.1), kind=kCustom, calls=%fused_computation.49 | custom fusion | bytes 524290 | tf_op jit(solution)/shard_map/scatter | solution.py:130
  168.7 10.5 %all-to-all-start.1 = ((bf16[128,8,256]{2,1,0:T(8,128)(2,1)}), bf16[128,8,256]{2,1,0:T(8,128)(2,1)S(1)}, u32[]{:S(2)}, u32[]{:S(2)}) async-start(bf16[128,8,256]{2,1,0:T(8,128)(2,1)} %bitcast.29), calls=%async_computation.1 | async-start | bytes 1048576 | tf_op jit(solution)/shard_map/all_to_all | solution.py:56
  179.2 3.2 %reduce = s32[128]{0:T(128)S(1)} reduce(s32[128,1,1]{2,1,0:T(1,128)} %all-to-all-done, s32[]{:T(128)} %constant.58.clone.1), dimensions={1,2}, to_apply=%all_to_all.10.reduce_sub_computation | reduce | bytes 1028 | tf_op jit(solution)/shard_map/all_to_all | solution.py:63
  182.6 10.4 %all-to-all-done.1 = bf16[128,8,256]{2,1,0:T(8,128)(2,1)S(1)} async-done(((bf16[128,8,256]{2,1,0:T(8,128)(2,1)}), bf16[128,8,256]{2,1,0:T(8,128)(2,1)S(1)}, u32[]{:S(2)}, u32[]{:S(2)}) %all-to-all-start.1) | async-done | bytes 524320 | tf_op jit(solution)/shard_map/all_to_all | solution.py:56
  193.0 7.0 %scatter_custom_fusion.1 = bf16[1024,256]{1,0:T(8,128)(2,1)} fusion(s32[1024]{0:T(1024)S(1)} %bitcast.97, bf16[128,8,256]{2,1,0:T(8,128)(2,1)S(1)} %all-to-all-done.1, bf16[]{:T(256)} %constant.53.clone.1), kind=kCustom, calls=%fused_computation.42 | custom fusion | flops 262144 | bytes 1048578 | tf_op jit(solution)/shard_map/scatter-add | solution.py:137
  (210 shorter events, 28.7 us)
Async XLA Ops:
  0.6 158.1 %copy-start = (bf16[512,256]{1,0:T(8,128)(2,1)S(1)}, bf16[512,256]{1,0:T(8,128)(2,1)}, u32[]{:S(2)}) copy-start(bf16[512,256]{1,0:T(8,128)(2,1)} %param.15) | copy-start | bytes 786436
  1.8 69.8 %collective-permute-start = (bf16[2,8,160,128]{3,2,1,0:T(8,128)(2,1)S(1)}, bf16[2,8,160,128]{3,2,1,0:T(8,128)(2,1)}, u32[]{:S(2)}, u32[]{:S(2)}) collective-permute-start(bf16[2,8,160,128]{3,2,1,0:T(8,128)(2,1)S(1)} %slice.76), channel_id=1, source_target_pairs={{0,4},{4,8},{8,12},{12,16},{16,20},{20,24},{24,28},{28,32},{32,36}... | collective-permute-start | bytes 1966088 | tf_op jit(solution)/shard_map/ppermute | solution.py:17
  9.6 61.3 %copy-start.13 = (s32[4,4,80]{2,1,0:T(4,128)S(1)}, s32[4,4,80]{2,1,0:T(4,128)}, u32[]{:S(2)}) copy-start(s32[4,4,80]{2,1,0:T(4,128)} %param.18) | copy-start | bytes 15364
  9.7 63.0 %copy-start.8 = (bf16[4,8,160,128]{3,2,1,0:T(8,128)(2,1)S(1)}, bf16[4,8,160,128]{3,2,1,0:T(8,128)(2,1)}, u32[]{:S(2)}) copy-start(bf16[4,8,160,128]{3,2,1,0:T(8,128)(2,1)} %param.11) | copy-start | bytes 3932164
  57.5 20.1 %copy-start.11 = (s32[4,4,80]{2,1,0:T(4,128)S(1)}, s32[4,4,80]{2,1,0:T(4,128)}, u32[]{:S(2)}) copy-start(s32[4,4,80]{2,1,0:T(4,128)} %param.19) | copy-start | bytes 15364
  63.4 105.3 %all-to-all-start = ((s32[128,1,1]{2,1,0:T(1,128)}), s32[128,1,1]{2,1,0:T(1,128)}, u32[]{:S(2)}, u32[]{:S(2)}) async-start(s32[128,1,1]{2,1,0:T(1,128)} %copy.47), calls=%async_computation | async-start | bytes 131072 | tf_op jit(solution)/shard_map/all_to_all | solution.py:63
  73.0 8.3 %collective-permute-start.1 = (bf16[6,1,160,128]{3,2,1,0:T(8,128)(2,1)S(1)}, bf16[6,1,160,128]{3,2,1,0:T(8,128)(2,1)S(1)}, u32[]{:S(2)}, u32[]{:S(2)}) collective-permute-start(bf16[6,1,160,128]{3,2,1,0:T(8,128)(2,1)S(1)} %get-tuple-element.122), channel_id=1, source_target_pairs={{0,1},{1,2},{2,3},{4,5},{5,6},{6,7},{8,9},{9,10},{10,11},{12,13},{... | collective-permute-start | bytes 737288 | tf_op jit(solution)/shard_map/ppermute | solution.py:28
  76.3 8.8 %collective-permute-start.2 = (bf16[6,1,160,128]{3,2,1,0:T(8,128)(2,1)S(1)}, bf16[6,1,160,128]{3,2,1,0:T(8,128)(2,1)S(1)}, u32[]{:S(2)}, u32[]{:S(2)}) collective-permute-start(bf16[6,1,160,128]{3,2,1,0:T(8,128)(2,1)S(1)} %get-tuple-element.123), channel_id=1, source_target_pairs={{1,0},{2,1},{3,2},{5,4},{6,5},{7,6},{9,8},{10,9},{11,10},{13,12},{... | collective-permute-start | bytes 737288 | tf_op jit(solution)/shard_map/ppermute | solution.py:30
  91.5 24.0 %copy-start.10 = (bf16[3,3,3,128,128]{4,3,2,1,0:T(8,128)(2,1)S(1)}, bf16[3,3,3,128,128]{4,3,2,1,0:T(8,128)(2,1)}, u32[]{:S(2)}) copy-start(bf16[3,3,3,128,128]{4,3,2,1,0:T(8,128)(2,1)} %param.12) | copy-start | bytes 2654212
  115.5 3.5 %copy-start.6 = (bf16[4,8,160,384]{3,2,1,0:T(8,128)(2,1)S(1)}, bf16[4,8,160,384]{3,2,1,0:T(8,128)(2,1)}, u32[]{:S(2)}) copy-start(bf16[4,8,160,384]{3,2,1,0:T(8,128)(2,1)} %get-tuple-element.113) | copy-start | bytes 11796484
  119.0 2.1 %copy-start.5 = (bf16[4,8,160,384]{3,2,1,0:T(8,128)(2,1)S(1)}, bf16[4,8,160,384]{3,2,1,0:T(8,128)(2,1)}, u32[]{:S(2)}) copy-start(bf16[4,8,160,384]{3,2,1,0:T(8,128)(2,1)} %get-tuple-element.114) | copy-start | bytes 11796484
  121.1 2.1 %copy-start.4 = (bf16[4,8,160,384]{3,2,1,0:T(8,128)(2,1)S(1)}, bf16[4,8,160,384]{3,2,1,0:T(8,128)(2,1)}, u32[]{:S(2)}) copy-start(bf16[4,8,160,384]{3,2,1,0:T(8,128)(2,1)} %get-tuple-element.115) | copy-start | bytes 11796484
  123.2 2.1 %copy-start.3 = (bf16[4,8,160,384]{3,2,1,0:T(8,128)(2,1)S(1)}, bf16[4,8,160,384]{3,2,1,0:T(8,128)(2,1)}, u32[]{:S(2)}) copy-start(bf16[4,8,160,384]{3,2,1,0:T(8,128)(2,1)} %get-tuple-element.116) | copy-start | bytes 11796484
  125.4 2.1 %copy-start.2 = (bf16[4,8,160,384]{3,2,1,0:T(8,128)(2,1)S(1)}, bf16[4,8,160,384]{3,2,1,0:T(8,128)(2,1)}, u32[]{:S(2)}) copy-start(bf16[4,8,160,384]{3,2,1,0:T(8,128)(2,1)} %get-tuple-element.117) | copy-start | bytes 11796484
  127.5 2.1 %copy-start.1 = (bf16[4,8,160,384]{3,2,1,0:T(8,128)(2,1)S(1)}, bf16[4,8,160,384]{3,2,1,0:T(8,128)(2,1)}, u32[]{:S(2)}) copy-start(bf16[4,8,160,384]{3,2,1,0:T(8,128)(2,1)} %get-tuple-element.118) | copy-start | bytes 11796484
  132.3 2.7 %copy-start.7 = (bf16[4,8,160,384]{3,2,1,0:T(8,128)(2,1)S(1)}, bf16[4,8,160,384]{3,2,1,0:T(8,128)(2,1)}, u32[]{:S(2)}) copy-start(bf16[4,8,160,384]{3,2,1,0:T(8,128)(2,1)} %get-tuple-element.111) | copy-start | bytes 11796484
  145.3 10.8 %copy-start.15 = (f32[128]{0:T(128)S(1)}, f32[128]{0:T(128)}, u32[]{:S(2)}) copy-start(f32[128]{0:T(128)} %param.14) | copy-start | bytes 1540
  145.3 10.8 %copy-start.16 = (f32[128]{0:T(128)S(1)}, f32[128]{0:T(128)}, u32[]{:S(2)}) copy-start(f32[128]{0:T(128)} %param.13) | copy-start | bytes 1540
  158.2 1.1 copy-start.12
  158.2 1.1 copy-start.14
  159.3 40.7 %copy-start.9 = (bf16[1280,256]{1,0:T(8,128)(2,1)}, bf16[1280,256]{1,0:T(8,128)(2,1)S(1)}, u32[]{:S(2)}) copy-start(bf16[1280,256]{1,0:T(8,128)(2,1)S(1)} %convolution_convert_fusion) | copy-start | bytes 1966084
  168.7 24.2 %all-to-all-start.1 = ((bf16[128,8,256]{2,1,0:T(8,128)(2,1)}), bf16[128,8,256]{2,1,0:T(8,128)(2,1)S(1)}, u32[]{:S(2)}, u32[]{:S(2)}) async-start(bf16[128,8,256]{2,1,0:T(8,128)(2,1)} %bitcast.29), calls=%async_computation.1 | async-start | bytes 1048576 | tf_op jit(solution)/shard_map/all_to_all | solution.py:56
where the time goes:
time: 201 us; the launch traced here: 200 us
  local copies, waits for them, and re-layouts  54.4 us (27%)
  blocking collectives  53.8 us (27%)
  starting transfers between devices  26.4 us (13%)
  other arithmetic  24.2 us (12%)
  matrix products  20.2 us (10%)
  waiting for transfers between devices  17 us (8%)
  loops' own time  2.94 us (1%)
    all_gather x1, blocking collectives, carried_in(): everything = lax.all_gather(array, axis)  46.4 us
    slice x1, local copies, waits for them, and re-layouts, on_device(): widened[frame_tap:frame_tap + frames, row_tap:row_tap + rows]  24 us
    dot_general x9, matrix products, on_device(): jnp.dot(window, folded[frame_tap, row_tap], preferred_element_type=jnp.fl...  19 us
    all_to_all x1, starting transfers between devices, deliver(): lax.all_to_all(outgoing.reshape(owners, CAP, width_out), ('tm', 'height')...  10.5 us
    all_to_all x1, waiting for transfers between devices, deliver(): lax.all_to_all(outgoing.reshape(owners, CAP, width_out), ('tm', 'height')...  10.4 us
    scatter x1, local copies, waits for them, and re-layouts, on_device(): jnp.zeros((owners * CAP, width_out), jnp.bfloat16).at[slot]  8.71 us
    psum x1, blocking collectives, on_device(): totals, squared = lax.psum((totals, squared), 'height')  7.49 us
    scatter-add x1, other arithmetic, on_device(): routed = jnp.zeros((owners * CAP, width_out), jnp.bfloat16).at[spots].add...  6.97 us
  transfers between devices with their start and end apart: 5, of which 3 were waited for; matrix products, arithmetic and copies ran while one was open for 43% of the time, Pallas kernels for 0%

commit v1 on v0

v1 whole, which is shorter than its diff:
```python
import functools

import jax
import jax.numpy as jnp
from jax import lax
from jax.experimental import pallas as pl
from jax.experimental.pallas import tpu as pltpu
from jax.sharding import PartitionSpec as P

GROUPS = 32
LMAX = 8
CAP = 8
EPSILON = 1e-06
LANES = 128
EMPTY = 2.0**127
LIMIT = 2.0**126
MESH = pl.DeviceIdType.MESH
F32 = jnp.float32
BF16 = jnp.bfloat16


def dot(a, b):
    return jnp.dot(a, b, preferred_element_type=F32)


def dot_t(a, b, precision=None):
    return lax.dot_general(
        a, b, (((1,), (1,)), ((), ())), preferred_element_type=F32, precision=precision
    )


def iota(shape, dim):
    return lax.broadcasted_iota(jnp.int32, shape, dim)


def onehot(mask):
    return jnp.where(mask, 1.0, 0.0).astype(BF16)


def encode_kernel(
    ntm, nh, shapes,
    video, weight, gain, bias, down, table, keep, run, owner,
    latent_out, payload_out,
    xbuf, wbuf, hidden, stat, codes, routes, extra, lat, pay,
    in_sem, w_sem, halo_send, halo_recv, stat_send, stat_recv, out_sem,
):
    frames, rows, cols, chans, width = shapes
    half_rows, half_cols = rows // 2, cols // 2
    toks = frames * half_rows * half_cols
    owners = ntm * nh
    slots = owners * CAP
    me_t, me_h = lax.axis_index("tm"), lax.axis_index("height")
    next_t, last_t = lax.rem(me_t + 1, ntm), lax.rem(me_t + ntm - 1, ntm)
    up, down_h = lax.rem(me_h + nh - 1, nh), lax.rem(me_h + 1, nh)
    peers = [lax.rem(me_h + k, nh) for k in range(1, nh)]

    own = pltpu.make_async_copy(
        video, xbuf.at[pl.ds(2, frames), pl.ds(1, rows)], in_sem
    )
    own.start()
    wcopies = [
        pltpu.make_async_copy(
            weight.at[:, e], wbuf.at[:, :, pl.ds(e * chans, chans)], w_sem.at[e]
        )
        for e in range(3)
    ]
    for copy in wcopies:
        copy.start()

    barrier = pltpu.get_barrier_semaphore()
    sources = [(last_t, me_h), (last_t, up), (last_t, down_h)] + [(me_t, h) for h in peers]
    for t, h in sources:
        pl.semaphore_signal(
            barrier, inc=1, device_id={"tm": t, "height": h}, device_id_type=MESH
        )
    pl.semaphore_wait(barrier, len(sources))

    def halo(k, src, dst, t, h):
        return pltpu.make_async_remote_copy(
            src_ref=src, dst_ref=dst, send_sem=halo_send.at[k], recv_sem=halo_recv.at[k],
            device_id={"tm": t, "height": h}, device_id_type=MESH,
        )

    own_rows = pl.ds(1, rows)
    to_up = halo(0, video.at[:, 0], xbuf.at[pl.ds(2, frames), rows + 1], me_t, up)
    to_down = halo(1, video.at[:, rows - 1], xbuf.at[pl.ds(2, frames), 0], me_t, down_h)
    late = halo(2, video.at[frames - 1], xbuf.at[1, own_rows], next_t, me_h)
    early = halo(3, video.at[frames - 2], xbuf.at[0, own_rows], next_t, me_h)
    pair = pl.ds(frames - 2, 2)
    corner_up = halo(4, video.at[pair, 0], xbuf.at[pl.ds(0, 2), rows + 1], next_t, up)
    corner_down = halo(5, video.at[pair, rows - 1], xbuf.at[pl.ds(0, 2), 0], next_t, down_h)
    for copy in (late, to_up, to_down, early, corner_up, corner_down):
        copy.start()

    codes[...] = jnp.zeros(codes.shape, F32)
    for t in range(frames):
        kept = keep[t] == 1
        where_to = jnp.where(kept, owner[t], owners)
        codes[0, pl.ds(t * half_rows, half_rows), pl.ds(0, half_cols)] = where_to.astype(F32)
        codes[1, pl.ds(t * half_rows, half_rows), pl.ds(0, half_cols)] = (
            run[t] - 1
        ).astype(F32)
    lines = frames * half_rows
    wide = codes.shape[2]
    spread_at = onehot(iota((wide, toks), 0) == lax.rem(iota((wide, toks), 1), half_cols))
    mine = iota((lines, toks), 0) == iota((lines, toks), 1) // half_cols
    code = jnp.sum(
        jnp.where(mine, dot(codes[0].astype(BF16), spread_at), 0.0), axis=0, keepdims=True
    )
    length = jnp.sum(
        jnp.where(mine, dot(codes[1].astype(BF16), spread_at), 0.0), axis=0, keepdims=True
    )
    code_i, length_i = code.astype(jnp.int32), length.astype(jnp.int32)
    member = iota((owners, toks), 0) == code_i
    before_lane = onehot(iota((LANES, LANES), 0) < iota((LANES, LANES), 1))
    carry = jnp.zeros((owners, 1), F32)
    for k in range(toks // LANES):
        at = slice(k * LANES, (k + 1) * LANES)
        block = jnp.where(member[:, at], 1.0, 0.0)
        ahead = dot(block.astype(BF16), before_lane) + carry
        carry = carry + jnp.sum(block, axis=1, keepdims=True)
        rank = jnp.sum(ahead * block, axis=0, keepdims=True).astype(jnp.int32)
        slot = jnp.where(code_i[:, at] < owners, code_i[:, at] * CAP + rank, -1)
        routes[:, at] = onehot(iota((slots, LANES), 0) == slot)
    lanes_t = 4 * LMAX
    line = iota((lanes_t, toks), 0)
    which = onehot((lax.rem(line, LMAX) == length_i) | (line >= 3 * LMAX))
    part0 = table[...].astype(BF16)
    rest = table[...] - part0.astype(F32)
    part1 = rest.astype(BF16)
    part2 = (rest - part1.astype(F32)).astype(BF16)
    parts = jnp.concatenate(
        [part0.astype(F32), part1.astype(F32), part2.astype(F32), jnp.zeros((LMAX, width), F32)],
        axis=0,
    ).astype(BF16)
    picked = dot_t(routes[...], which)
    added = dot(picked.astype(BF16), parts)
    extra[...] = jnp.where(picked[:, 3 * LMAX : 3 * LMAX + 1] > 0.5, added, EMPTY)

    for copy in wcopies:
        copy.wait()
    own.wait()

    first = iota((1, cols, chans), 1) == 0
    final = iota((1, cols, chans), 1) == cols - 1

    def convolve(t, r0, count):
        window = jnp.concatenate(
            [
                xbuf[t + a, pl.ds(r0 + b, count)].reshape(count * cols, chans)
                for a in range(3)
                for b in range(3)
            ],
            axis=1,
        )
        taps = dot(window, wbuf[...].reshape(9 * chans, 3 * chans))
        left = pltpu.roll(taps[:, :chans], 1, 0).reshape(count, cols, chans)
        right = pltpu.roll(taps[:, 2 * chans :], count * cols - 1, 0).reshape(count, cols, chans)
        out = taps[:, chans : 2 * chans].reshape(count, cols, chans)
        out = out + jnp.where(first, 0.0, left) + jnp.where(final, 0.0, right)
        hidden[t, pl.ds(r0, count)] = out
        tiles = out.reshape(count * cols // 8, 8, chans)
        stat[me_h, t, pl.ds(0, 8)] += jnp.sum(tiles, axis=0)
        stat[me_h, t, pl.ds(8, 8)] += jnp.sum(tiles * tiles, axis=0)

    def clear_rows(at, count):
        @pl.when(me_h == 0)
        def _():
            xbuf[pl.ds(at, count), 0] = jnp.zeros((count, cols, chans), BF16)

        @pl.when(me_h == nh - 1)
        def _():
            xbuf[pl.ds(at, count), rows + 1] = jnp.zeros((count, cols, chans), BF16)

    def clear_frame(at):
        @pl.when(me_t == 0)
        def _():
            xbuf[at] = jnp.zeros((rows + 2, cols, chans), BF16)

    def stat_copy(t, k):
        return pltpu.make_async_remote_copy(
            src_ref=stat.at[me_h, t], dst_ref=stat.at[me_h, t],
            send_sem=stat_send.at[t, k], recv_sem=stat_recv.at[t, me_h],
            device_id={"tm": me_t, "height": peers[k]}, device_id_type=MESH,
        )

    def stat_arrival(t, k):
        return pltpu.make_async_remote_copy(
            src_ref=stat.at[peers[k], t], dst_ref=stat.at[peers[k], t],
            send_sem=stat_send.at[t, k], recv_sem=stat_recv.at[t, peers[k]],
            device_id={"tm": me_t, "height": peers[k]}, device_id_type=MESH,
        )

    step = 2

    def frame_conv(t):
        stat[me_h, t] = jnp.zeros(stat.shape[2:], F32)

        def some(i, _):
            convolve(t, i * step, step)
            return 0

        lax.fori_loop(0, rows // step, some, 0)
        for k in range(nh - 1):
            stat_copy(t, k).start()

    group_of = chans // GROUPS
    same = jnp.where(
        iota((chans, chans), 0) // group_of == iota((chans, chans), 1) // group_of, 1.0, 0.0
    )
    count = rows * nh * cols * group_of

    def finish(t):
        for k in range(nh - 1):
            stat_arrival(t, k).wait_recv()
        summed = jnp.sum(stat[:, t], axis=0).reshape(2, 8, chans)
        summed = jnp.sum(summed, axis=1)
        pads = jnp.concatenate([summed, jnp.zeros((6, chans), F32)], axis=0)
        grouped = jnp.dot(
            pads, same, preferred_element_type=F32, precision=lax.Precision.HIGHEST
        ) / count
        average, squares = grouped[0:1], grouped[1:2]
        spread = squares - average * average
        scale = lax.rsqrt(spread + EPSILON) * gain[...]

        def act(r, b):
            h = hidden[t, r, pl.ds(b, half_cols, stride=2), :]
            v = 0.5 * ((h - average) * scale + bias[...])
            return (v * (1.0 + jnp.tanh(v))).astype(BF16)

        for i in range(half_rows):
            merged = jnp.concatenate(
                [act(2 * i + a, b) for a in range(2) for b in range(2)], axis=1
            )
            lat[t * half_rows + i] = dot(merged, down[...]).astype(BF16)
        pltpu.make_async_copy(
            lat.at[pl.ds(t * half_rows, half_rows)], latent_out.at[t], out_sem.at[t]
        ).start()

    to_up.wait_recv()
    to_down.wait_recv()
    clear_rows(2, frames)
    for t in range(frames - 1, 1, -1):
        frame_conv(t)
    late.wait_recv()
    early.wait_recv()
    corner_up.wait_recv()
    corner_down.wait_recv()
    clear_rows(0, 2)
    clear_frame(0)
    clear_frame(1)
    frame_conv(1)
    frame_conv(0)
    for t in range(frames - 1, -1, -1):
        finish(t)
    out = dot(routes[...], lat[...].reshape(toks, width)) + extra[...]
    sides = [
        out[:, k * LANES : (k + 1) * LANES].reshape(owners, CAP, LANES)
        for k in range(width // LANES)
    ]
    pay[...] = jnp.concatenate(sides, axis=1).astype(BF16)
    leave = pltpu.make_async_copy(pay, payload_out, out_sem.at[frames])
    leave.start()
    for copy in (late, to_up, to_down, early, corner_up, corner_down):
        copy.wait_send()
    for t in range(frames):
        for k in range(nh - 1):
            stat_copy(t, k).wait_send()
        pltpu.make_async_copy(
            lat.at[pl.ds(t * half_rows, half_rows)], latent_out.at[t], out_sem.at[t]
        ).wait()
    leave.wait()


def compact(arrived, owners, width):
    slots = owners * CAP
    block = min(LANES, slots)
    tall = arrived.astype(F32)
    sides = [
        tall[:, k * CAP : (k + 1) * CAP].reshape(slots, LANES) for k in range(width // LANES)
    ]
    rows = jnp.concatenate(sides, axis=1).astype(BF16)
    pick = onehot(iota((8, LANES), 1) == 0)
    lead = dot_t(pick, sides[0].astype(BF16))
    ahead_of = onehot(iota((block, block), 0) < iota((block, block), 1))
    carry = jnp.zeros((8, 1), F32)
    places = []
    for k in range(slots // block):
        valid = jnp.where(lead[:, k * block : (k + 1) * block] < LIMIT, 1.0, 0.0)
        place = dot(valid.astype(BF16), ahead_of) + carry
        carry = carry + jnp.sum(valid, axis=1, keepdims=True)
        places.append(jnp.where(valid > 0.5, place, -1.0)[0:1].astype(jnp.int32))
    chosen = jnp.concatenate(
        [onehot(iota((slots, block), 0) == place) for place in places], axis=1
    )
    return dot(chosen, rows).astype(BF16)


def compact_kernel(owners, width, arrived, routed):
    routed[...] = compact(arrived[...], owners, width)


def on_device(
    ntm, nh, video, conv_weight, norm_gain, norm_bias, down_weight, length_table, keep, run_length, owner
):
    frames, rows, cols, chans = video.shape
    width = down_weight.shape[1]
    half_rows, half_cols = rows // 2, cols // 2
    toks = frames * half_rows * half_cols
    owners = ntm * nh
    slots = owners * CAP
    any_spec = pl.BlockSpec(memory_space=pl.ANY)
    vmem = pl.BlockSpec(memory_space=pltpu.VMEM)
    tiles = CAP * width // LANES
    latent, payload = pl.pallas_call(
        functools.partial(encode_kernel, ntm, nh, (frames, rows, cols, chans, width)),
        out_shape=(
            jax.ShapeDtypeStruct((frames, half_rows, half_cols, width), BF16),
            jax.ShapeDtypeStruct((owners, tiles, LANES), BF16),
        ),
        in_specs=[any_spec, any_spec] + [vmem] * 7,
        out_specs=(any_spec, any_spec),
        scratch_shapes=[
            pltpu.VMEM((frames + 2, rows + 2, cols, chans), BF16),
            pltpu.VMEM((9, chans, 3 * chans), BF16),
            pltpu.VMEM((frames, rows, cols, chans), F32),
            pltpu.VMEM((nh, frames, 16, chans), F32),
            pltpu.VMEM((2, frames * half_rows, LANES), F32),
            pltpu.VMEM((slots, toks), BF16),
            pltpu.VMEM((slots, width), F32),
            pltpu.VMEM((frames * half_rows, half_cols, width), BF16),
            pltpu.VMEM((owners, tiles, LANES), BF16),
            pltpu.SemaphoreType.DMA,
            pltpu.SemaphoreType.DMA((3,)),
            pltpu.SemaphoreType.DMA((6,)),
            pltpu.SemaphoreType.DMA((6,)),
            pltpu.SemaphoreType.DMA((frames, nh - 1)),
            pltpu.SemaphoreType.DMA((frames, nh)),
            pltpu.SemaphoreType.DMA((frames + 1,)),
        ],
        compiler_params=pltpu.CompilerParams(
            collective_id=0, has_side_effects=True, vmem_limit_bytes=48 * 1024 * 1024
        ),
        name="encode",
    )(
        video,
        conv_weight.reshape(9, 3, chans, chans),
        norm_gain.reshape(1, chans),
        norm_bias.reshape(1, chans),
        down_weight,
        length_table,
        keep,
        run_length,
        owner,
    )
    arrived = lax.all_to_all(
        payload, ("tm", "height"), split_axis=0, concat_axis=0, tiled=True
    )
    routed = pl.pallas_call(
        functools.partial(compact_kernel, owners, width),
        out_shape=jax.ShapeDtypeStruct((slots, width), BF16),
        in_specs=[vmem],
        out_specs=vmem,
        compiler_params=pltpu.CompilerParams(vmem_limit_bytes=48 * 1024 * 1024),
        name="compact",
    )(arrived)
    return latent, routed


def solution(mesh):
    return jax.shard_map(
        functools.partial(on_device, mesh.shape["tm"], mesh.shape["height"]),
        mesh=mesh,
        in_specs=(
            P("tm", "height", None, None),
            P(),
            P(),
            P(),
            P(),
            P(),
            P("tm", "height", None),
            P("tm", "height", None),
            P("tm", "height", None),
        ),
        out_specs=(P("tm", "height", None, None), P(("tm", "height"), None)),
        check_vma=False,
    )
```

time: 201 us -> 61.6 us (0.31)
  blocking collectives: 53.8 us -> 0 us
  local copies, waits for them, and re-layouts: 54.4 us -> 8.36 us
  Pallas kernels: 0 us -> 28.6 us
  other arithmetic: 24.2 us -> 0 us
  matrix products: 20.2 us -> 0 us
  starting transfers between devices: 26.4 us -> 9.7 us
  waiting for transfers between devices: 17 us -> 13.8 us
  loops' own time: 2.94 us -> 0 us
    all_gather x1 -> x0, blocking collectives: 46.4 us -> none  [carried_in(): everything = lax.all_gather(array, axis)]
    pallas_call x0 -> x2, Pallas kernels: none -> 28.6 us  [the longest x1 26.9 us: on_device(): pl.pallas_call(functools.partial(encode_kernel, ntm, nh, (frames, rows, c...]
    slice x4 -> x0, local copies, waits for them, and re-layouts: 26.8 us -> none  [the longest x1 24 us: on_device(): widened[frame_tap:frame_tap + frames, row_tap:row_tap + rows]]
    dot_general x11 -> x0, matrix products: 20.2 us -> none  [the longest x9 19 us: on_device(): jnp.dot(window, folded[frame_tap, row_tap], preferred_element_type=jnp.fl...]
    ppermute x3 -> x0, starting transfers between devices: 9.11 us -> none  [the longest x1 4.51 us: passed_along(): return lax.ppermute(block, axis, route)]
    scatter x1 -> x0, local copies, waits for them, and re-layouts: 8.71 us -> none  [on_device(): jnp.zeros((owners * CAP, width_out), jnp.bfloat16).at[slot]]
    all_to_all x2 -> x1, starting transfers between devices: 17.3 us -> 9.7 us  [on_device(): lax.all_to_all(payload, ('tm', 'height'), split_axis=0, concat_axis=0, ti...]
    psum x1 -> x0, blocking collectives: 7.49 us -> none  [on_device(): totals, squared = lax.psum((totals, squared), 'height')]
  transfers between devices with their start and end apart: 5 -> 1, of which waited for: 3 -> 1; matrix products, arithmetic and copies ran while one was open for 43% -> 0% of each run, Pallas kernels for 0% -> 0%
where the time goes in v1:
time: 61.6 us; the launch traced here: 61.1 us
  Pallas kernels  28.6 us (46%)
  waiting for transfers between devices  13.8 us (22%)
  starting transfers between devices  9.7 us (16%)
  local copies, waits for them, and re-layouts  8.36 us (14%)
  between operations  0.67 us (1%)
    pallas_call x1, Pallas kernels, on_device(): pl.pallas_call(functools.partial(encode_kernel, ntm, nh, (frames, rows, c...  26.9 us
    all_to_all x1, waiting for transfers between devices, on_device(): lax.all_to_all(payload, ('tm', 'height'), split_axis=0, concat_axis=0, ti...  13.8 us
    all_to_all x1, starting transfers between devices, on_device(): lax.all_to_all(payload, ('tm', 'height'), split_axis=0, concat_axis=0, ti...  9.7 us
    unnamed x19, local copies, waits for them, and re-layouts  8.36 us
    pallas_call x1, Pallas kernels, on_device(): pl.pallas_call(functools.partial(compact_kernel, owners, width), out_shap...  1.76 us
  transfers between devices with their start and end apart: 1, of which 1 were waited for; matrix products, arithmetic and copies ran while one was open for 0% of the time, Pallas kernels for 0%

profile of v1, /device:TPU:1, one launch (start us, length us, event | category | flops | bytes accessed | tf_op | source)
XLA Modules:
  0.0 61.1 jit_solution(6406768102120581356)
XLA Ops:
  0.6 0.0 copy-start
  0.6 1.3 %copy-done = bf16[4,8,160,128]{3,2,1,0:T(8,128)(2,1)S(1)} copy-done((bf16[4,8,160,128]{3,2,1,0:T(8,128)(2,1)S(1)}, bf16[4,8,160,128]{3,2,1,0:T(8,128)(2,1)}, u32[]{:S(2)}) %copy-start) | copy-done | bytes 1310744
  2.0 0.0 copy-start.1
  2.0 1.2 %copy-done.1 = bf16[3,3,3,128,128]{4,3,2,1,0:T(8,128)(2,1)S(1)} copy-done((bf16[3,3,3,128,128]{4,3,2,1,0:T(8,128)(2,1)S(1)}, bf16[3,3,3,128,128]{4,3,2,1,0:T(8,128)(2,1)}, u32[]{:S(2)}) %copy-start.1) | copy-done | bytes 884760
  3.1 0.0 copy-start.2
  3.1 0.9 %copy-done.2 = bf16[512,256]{1,0:T(8,128)(2,1)S(1)} copy-done((bf16[512,256]{1,0:T(8,128)(2,1)S(1)}, bf16[512,256]{1,0:T(8,128)(2,1)}, u32[]{:S(2)}) %copy-start.2) | copy-done | bytes 262168
  4.1 0.0 copy-start.3
  4.1 0.7 %copy-done.3 = f32[8,256]{1,0:T(8,128)S(1)} copy-done((f32[8,256]{1,0:T(8,128)S(1)}, f32[8,256]{1,0:T(8,128)}, u32[]{:S(2)}) %copy-start.3) | copy-done | bytes 8216
  4.8 0.0 copy-start.4
  4.8 0.7 %copy-done.4 = s32[4,4,80]{2,1,0:T(4,128)S(1)} copy-done((s32[4,4,80]{2,1,0:T(4,128)S(1)}, s32[4,4,80]{2,1,0:T(4,128)}, u32[]{:S(2)}) %copy-start.4) | copy-done | bytes 5144
  5.5 0.0 copy-start.5
  5.5 0.7 %copy-done.5 = s32[4,4,80]{2,1,0:T(4,128)S(1)} copy-done((s32[4,4,80]{2,1,0:T(4,128)S(1)}, s32[4,4,80]{2,1,0:T(4,128)}, u32[]{:S(2)}) %copy-start.5) | copy-done | bytes 5144
  6.2 0.0 copy-start.6
  6.2 0.7 %copy-done.6 = s32[4,4,80]{2,1,0:T(4,128)S(1)} copy-done((s32[4,4,80]{2,1,0:T(4,128)S(1)}, s32[4,4,80]{2,1,0:T(4,128)}, u32[]{:S(2)}) %copy-start.6) | copy-done | bytes 5144
  6.9 0.0 copy-start.7
  6.9 0.7 %copy-done.7 = f32[128]{0:T(128)S(1)} copy-done((f32[128]{0:T(128)S(1)}, f32[128]{0:T(128)}, u32[]{:S(2)}) %copy-start.7) | copy-done | bytes 536
  7.5 0.0 copy-start.8
  7.5 0.7 %copy-done.8 = f32[128]{0:T(128)S(1)} copy-done((f32[128]{0:T(128)S(1)}, f32[128]{0:T(128)}, u32[]{:S(2)}) %copy-start.8) | copy-done | bytes 536
  8.2 26.9 %encode.1 = (bf16[4,4,80,256]{3,2,1,0:T(8,128)(2,1)S(1)}, bf16[128,16,128]{2,1,0:T(8,128)(2,1)}) custom-call(bf16[4,8,160,128]{3,2,1,0:T(8,128)(2,1)S(1)} %copy-done, bf16[9,3,128,128]{3,2,1,0:T(8,128)(2,1)S(1)} %bitcast.3, f32[1,128]{1,0:T(1,128)S(1)} %bitcast.4, f32[1,128]{1,0:T(1,128)S(1)} %bitcast.5, bf16[512,256]{1,0:T(8,128)(2,1)S(1)} %copy-done.2, ...), custom_call_target="tpu_custom_call" | custom-call | tf_op jit(solution)/shard_map/encode/pallas_call | solution.py:315
  35.1 9.7 %all-to-all-start = ((bf16[128,16,128]{2,1,0:T(8,128)(2,1)}), bf16[128,16,128]{2,1,0:T(8,128)(2,1)S(1)}, u32[]{:S(2)}, u32[]{:S(2)}) async-start(bf16[128,16,128]{2,1,0:T(8,128)(2,1)} %get-tuple-element.5), calls=%async_computation | async-start | bytes 1048576 | tf_op jit(solution)/shard_map/all_to_all | solution.py:356
  44.8 13.8 %all-to-all-done.arrived = bf16[128,16,128]{2,1,0:T(8,128)(2,1)S(1)} async-done(((bf16[128,16,128]{2,1,0:T(8,128)(2,1)}), bf16[128,16,128]{2,1,0:T(8,128)(2,1)S(1)}, u32[]{:S(2)}, u32[]{:S(2)}) %all-to-all-start) | async-done | bytes 524320 | tf_op jit(solution)/shard_map/all_to_all | solution.py:356
  58.5 1.8 %compact.1 = bf16[1024,256]{1,0:T(8,128)(2,1)} custom-call(bf16[128,16,128]{2,1,0:T(8,128)(2,1)S(1)} %all-to-all-done.arrived), custom_call_target="tpu_custom_call" | custom-call | tf_op jit(solution)/shard_map/compact/pallas_call | solution.py:359
  60.3 0.8 %copy.12 = bf16[4,4,80,256]{3,2,1,0:T(8,128)(2,1)} copy(bf16[4,4,80,256]{3,2,1,0:T(8,128)(2,1)S(1)} %get-tuple-element.8) | data formatting | bytes 1310720
Async XLA Ops:
  0.6 1.3 %copy-start = (bf16[4,8,160,128]{3,2,1,0:T(8,128)(2,1)S(1)}, bf16[4,8,160,128]{3,2,1,0:T(8,128)(2,1)}, u32[]{:S(2)}) copy-start(bf16[4,8,160,128]{3,2,1,0:T(8,128)(2,1)} %video.1) | copy-start | bytes 3932164
  2.0 1.2 %copy-start.1 = (bf16[3,3,3,128,128]{4,3,2,1,0:T(8,128)(2,1)S(1)}, bf16[3,3,3,128,128]{4,3,2,1,0:T(8,128)(2,1)}, u32[]{:S(2)}) copy-start(bf16[3,3,3,128,128]{4,3,2,1,0:T(8,128)(2,1)} %param.10) | copy-start | bytes 2654212
  3.1 0.9 %copy-start.2 = (bf16[512,256]{1,0:T(8,128)(2,1)S(1)}, bf16[512,256]{1,0:T(8,128)(2,1)}, u32[]{:S(2)}) copy-start(bf16[512,256]{1,0:T(8,128)(2,1)} %down.1) | copy-start | bytes 786436
  4.1 0.7 %copy-start.3 = (f32[8,256]{1,0:T(8,128)S(1)}, f32[8,256]{1,0:T(8,128)}, u32[]{:S(2)}) copy-start(f32[8,256]{1,0:T(8,128)} %table.1) | copy-start | bytes 24580
  4.8 0.7 %copy-start.4 = (s32[4,4,80]{2,1,0:T(4,128)S(1)}, s32[4,4,80]{2,1,0:T(4,128)}, u32[]{:S(2)}) copy-start(s32[4,4,80]{2,1,0:T(4,128)} %keep.1) | copy-start | bytes 15364
  5.5 0.7 %copy-start.5 = (s32[4,4,80]{2,1,0:T(4,128)S(1)}, s32[4,4,80]{2,1,0:T(4,128)}, u32[]{:S(2)}) copy-start(s32[4,4,80]{2,1,0:T(4,128)} %run.1) | copy-start | bytes 15364
  6.2 0.7 %copy-start.6 = (s32[4,4,80]{2,1,0:T(4,128)S(1)}, s32[4,4,80]{2,1,0:T(4,128)}, u32[]{:S(2)}) copy-start(s32[4,4,80]{2,1,0:T(4,128)} %owner.1) | copy-start | bytes 15364
  6.9 0.7 %copy-start.7 = (f32[128]{0:T(128)S(1)}, f32[128]{0:T(128)}, u32[]{:S(2)}) copy-start(f32[128]{0:T(128)} %param.11) | copy-start | bytes 1540
  7.5 0.7 %copy-start.8 = (f32[128]{0:T(128)S(1)}, f32[128]{0:T(128)}, u32[]{:S(2)}) copy-start(f32[128]{0:T(128)} %param.12) | copy-start | bytes 1540
  35.1 23.5 %all-to-all-start = ((bf16[128,16,128]{2,1,0:T(8,128)(2,1)}), bf16[128,16,128]{2,1,0:T(8,128)(2,1)S(1)}, u32[]{:S(2)}, u32[]{:S(2)}) async-start(bf16[128,16,128]{2,1,0:T(8,128)(2,1)} %get-tuple-element.5), calls=%async_computation | async-start | bytes 1048576 | tf_op jit(solution)/shard_map/all_to_all | solution.py:356

commit v2 on v1

--- a/solution.py
+++ b/solution.py
@@ -38,11 +38,12 @@
 
 
 def encode_kernel(
-    ntm, nh, shapes,
-    video, weight, gain, bias, down, table, keep, run, owner,
-    latent_out, payload_out,
-    xbuf, wbuf, hidden, stat, codes, routes, extra, lat, pay,
-    in_sem, w_sem, halo_send, halo_recv, stat_send, stat_recv, out_sem,
+    ntm, nh, shapes, ways,
+    video_in, weight_in, gain_in, bias_in, down_in, table_in, keep_in, run_in, owner_in,
+    latent_out, arrived,
+    xbuf, wpair, wlast, gain, bias, down, table, keep, run, owner,
+    hidden, stat, codes, routes, extra, lat, pay,
+    in_sem, halo_send, halo_recv, stat_send, stat_recv, ready, out_sem, go_sem, come_sem,
 ):
     frames, rows, cols, chans, width = shapes
     half_rows, half_cols = rows // 2, cols // 2
@@ -50,29 +51,42 @@
     owners = ntm * nh
     slots = owners * CAP
     me_t, me_h = lax.axis_index("tm"), lax.axis_index("height")
+    me = me_t * nh + me_h
     next_t, last_t = lax.rem(me_t + 1, ntm), lax.rem(me_t + ntm - 1, ntm)
     up, down_h = lax.rem(me_h + nh - 1, nh), lax.rem(me_h + 1, nh)
     peers = [lax.rem(me_h + k, nh) for k in range(1, nh)]
 
-    own = pltpu.make_async_copy(
-        video, xbuf.at[pl.ds(2, frames), pl.ds(1, rows)], in_sem
-    )
-    own.start()
-    wcopies = [
-        pltpu.make_async_copy(
-            weight.at[:, e], wbuf.at[:, :, pl.ds(e * chans, chans)], w_sem.at[e]
-        )
-        for e in range(3)
+    fast, slow = ways
+    plane, line = me_t // fast, lax.rem(me_t, fast)
+    rounds = [
+        [(me_t, h) for h in peers],
+        [(plane * fast + lax.rem(line + k, fast), me_h) for k in range(1, fast)],
+        [(lax.rem(plane + k, slow) * fast + line, me_h) for k in range(1, slow)],
     ]
-    for copy in wcopies:
-        copy.start()
-
+    sources = [(last_t, me_h), (last_t, up), (last_t, down_h)]
+    sources += [target for group in rounds for target in group]
     barrier = pltpu.get_barrier_semaphore()
-    sources = [(last_t, me_h), (last_t, up), (last_t, down_h)] + [(me_t, h) for h in peers]
     for t, h in sources:
         pl.semaphore_signal(
             barrier, inc=1, device_id={"tm": t, "height": h}, device_id_type=MESH
         )
+
+    loads = [
+        (keep_in, keep), (run_in, run), (owner_in, owner), (table_in, table),
+        (video_in, xbuf.at[pl.ds(2, frames), pl.ds(1, rows)]),
+        (weight_in.at[:, :, 0], wpair.at[:, :, :, pl.ds(0, chans)]),
+        (weight_in.at[:, :, 1], wpair.at[:, :, :, pl.ds(chans, chans)]),
+        (weight_in.at[:, :, 2], wlast.at[:, pl.ds(0, 3), :, pl.ds(0, chans)]),
+        (weight_in.at[:, :, 2], wlast.at[:, pl.ds(1, 3), :, pl.ds(chans, chans)]),
+        (down_in, down), (gain_in, gain), (bias_in, bias),
+    ]
+    loads = [
+        pltpu.make_async_copy(src, dst, in_sem.at[k]) for k, (src, dst) in enumerate(loads)
+    ]
+    for copy in loads:
+        copy.start()
+    wlast[:, 3, :, pl.ds(0, chans)] = jnp.zeros((3, chans, chans), BF16)
+    wlast[:, 0, :, pl.ds(chans, chans)] = jnp.zeros((3, chans, chans), BF16)
     pl.semaphore_wait(barrier, len(sources))
 
     def halo(k, src, dst, t, h):
@@ -82,16 +96,30 @@
         )
 
     own_rows = pl.ds(1, rows)
-    to_up = halo(0, video.at[:, 0], xbuf.at[pl.ds(2, frames), rows + 1], me_t, up)
-    to_down = halo(1, video.at[:, rows - 1], xbuf.at[pl.ds(2, frames), 0], me_t, down_h)
-    late = halo(2, video.at[frames - 1], xbuf.at[1, own_rows], next_t, me_h)
-    early = halo(3, video.at[frames - 2], xbuf.at[0, own_rows], next_t, me_h)
+    to_up = halo(0, video_in.at[:, 0], xbuf.at[pl.ds(2, frames), rows + 1], me_t, up)
+    to_down = halo(1, video_in.at[:, rows - 1], xbuf.at[pl.ds(2, frames), 0], me_t, down_h)
+    late = halo(2, video_in.at[frames - 1], xbuf.at[1, own_rows], next_t, me_h)
+    early = halo(3, video_in.at[frames - 2], xbuf.at[0, own_rows], next_t, me_h)
     pair = pl.ds(frames - 2, 2)
-    corner_up = halo(4, video.at[pair, 0], xbuf.at[pl.ds(0, 2), rows + 1], next_t, up)
-    corner_down = halo(5, video.at[pair, rows - 1], xbuf.at[pl.ds(0, 2), 0], next_t, down_h)
-    for copy in (late, to_up, to_down, early, corner_up, corner_down):
+    corner_up = halo(4, video_in.at[pair, 0], xbuf.at[pl.ds(0, 2), rows + 1], next_t, up)
+    corner_down = halo(5, video_in.at[pair, rows - 1], xbuf.at[pl.ds(0, 2), 0], next_t, down_h)
+    halos = (late, to_up, to_down, early, corner_up, corner_down)
+    for copy in halos:
         copy.start()
 
+    def tell(k):
+        for t, h in rounds[k]:
+            pl.semaphore_signal(
+                ready.at[k], inc=1, device_id={"tm": t, "height": h}, device_id_type=MESH
+            )
+
+    def hear(k):
+        if rounds[k]:
+            pl.semaphore_wait(ready.at[k], len(rounds[k]))
+
+    tell(0)
+    for copy in loads[:4]:
+        copy.wait()
     codes[...] = jnp.zeros(codes.shape, F32)
     for t in range(frames):
         kept = keep[t] == 1
@@ -123,8 +151,8 @@
         slot = jnp.where(code_i[:, at] < owners, code_i[:, at] * CAP + rank, -1)
         routes[:, at] = onehot(iota((slots, LANES), 0) == slot)
     lanes_t = 4 * LMAX
-    line = iota((lanes_t, toks), 0)
-    which = onehot((lax.rem(line, LMAX) == length_i) | (line >= 3 * LMAX))
+    row_of = iota((lanes_t, toks), 0)
+    which = onehot((lax.rem(row_of, LMAX) == length_i) | (row_of >= 3 * LMAX))
     part0 = table[...].astype(BF16)
     rest = table[...] - part0.astype(F32)
     part1 = rest.astype(BF16)
@@ -137,14 +165,16 @@
     added = dot(picked.astype(BF16), parts)
     extra[...] = jnp.where(picked[:, 3 * LMAX : 3 * LMAX + 1] > 0.5, added, EMPTY)
 
-    for copy in wcopies:
+    for copy in loads[4:]:
         copy.wait()
-    own.wait()
+    hear(0)
+    tell(1)
 
     first = iota((1, cols, chans), 1) == 0
     final = iota((1, cols, chans), 1) == cols - 1
 
     def convolve(t, r0, count):
+        half = count // 2
         window = jnp.concatenate(
             [
                 xbuf[t + a, pl.ds(r0 + b, count)].reshape(count * cols, chans)
@@ -153,15 +183,32 @@
             ],
             axis=1,
         )
-        taps = dot(window, wbuf[...].reshape(9 * chans, 3 * chans))
+        taps = dot(window, wpair[...].reshape(9 * chans, 2 * chans))
         left = pltpu.roll(taps[:, :chans], 1, 0).reshape(count, cols, chans)
-        right = pltpu.roll(taps[:, 2 * chans :], count * cols - 1, 0).reshape(count, cols, chans)
-        out = taps[:, chans : 2 * chans].reshape(count, cols, chans)
-        out = out + jnp.where(first, 0.0, left) + jnp.where(final, 0.0, right)
+        out = taps[:, chans:].reshape(count, cols, chans) + jnp.where(first, 0.0, left)
+        window = jnp.concatenate(
+            [
+                jnp.concatenate([xbuf[t + a, r0 + b + 2 * i] for i in range(half)], axis=0)
+                for a in range(3)
+                for b in range(4)
+            ],
+            axis=1,
+        )
+        taps = dot(window, wlast[...].reshape(12 * chans, 2 * chans))
+        right = jnp.concatenate(
+            [
+                pltpu.roll(taps[:, k * chans : (k + 1) * chans], half * cols - 1, 0).reshape(
+                    half, 1, cols, chans
+                )
+                for k in range(2)
+            ],
+            axis=1,
+        ).reshape(count, cols, chans)
+        out = out + jnp.where(final, 0.0, right)
         hidden[t, pl.ds(r0, count)] = out
         tiles = out.reshape(count * cols // 8, 8, chans)
-        stat[me_h, t, pl.ds(0, 8)] += jnp.sum(tiles, axis=0)
-        stat[me_h, t, pl.ds(8, 8)] += jnp.sum(tiles * tiles, axis=0)
+        stat[me_h, t, pl.ds(0, 8)] = jnp.sum(tiles, axis=0)
+        stat[me_h, t, pl.ds(8, 8)] = jnp.sum(tiles * tiles, axis=0)
 
     def clear_rows(at, count):
         @pl.when(me_h == 0)
@@ -171,11 +218,6 @@
         @pl.when(me_h == nh - 1)
         def _():
             xbuf[pl.ds(at, count), rows + 1] = jnp.zeros((count, cols, chans), BF16)
-
-    def clear_frame(at):
-        @pl.when(me_t == 0)
-        def _():
-            xbuf[at] = jnp.zeros((rows + 2, cols, chans), BF16)
 
     def stat_copy(t, k):
         return pltpu.make_async_remote_copy(
@@ -191,16 +233,8 @@
             device_id={"tm": me_t, "height": peers[k]}, device_id_type=MESH,
         )
 
-    step = 2
-
     def frame_conv(t):
-        stat[me_h, t] = jnp.zeros(stat.shape[2:], F32)
-
-        def some(i, _):
-            convolve(t, i * step, step)
-            return 0
-
-        lax.fori_loop(0, rows // step, some, 0)
+        convolve(t, 0, rows)
         for k in range(nh - 1):
             stat_copy(t, k).start()
 
@@ -228,48 +262,76 @@
             v = 0.5 * ((h - average) * scale + bias[...])
             return (v * (1.0 + jnp.tanh(v))).astype(BF16)
 
-        for i in range(half_rows):
-            merged = jnp.concatenate(
-                [act(2 * i + a, b) for a in range(2) for b in range(2)], axis=1
-            )
-            lat[t * half_rows + i] = dot(merged, down[...]).astype(BF16)
-        pltpu.make_async_copy(
+        merged = jnp.concatenate(
+            [
+                jnp.concatenate(
+                    [act(2 * i + a, b) for a in range(2) for b in range(2)], axis=1
+                )
+                for i in range(half_rows)
+            ],
+            axis=0,
+        )
+        lat[pl.ds(t * half_rows, half_rows)] = (
+            dot(merged, down[...]).astype(BF16).reshape(half_rows, half_cols, width)
+        )
+        latent_copy(t).start()
+
+    def latent_copy(t):
+        return pltpu.make_async_copy(
             lat.at[pl.ds(t * half_rows, half_rows)], latent_out.at[t], out_sem.at[t]
-        ).start()
+        )
 
     to_up.wait_recv()
     to_down.wait_recv()
     clear_rows(2, frames)
     for t in range(frames - 1, 1, -1):
         frame_conv(t)
+    hear(1)
+    tell(2)
     late.wait_recv()
-    early.wait_recv()
     corner_up.wait_recv()
     corner_down.wait_recv()
+    early.wait_recv()
     clear_rows(0, 2)
-    clear_frame(0)
-    clear_frame(1)
+
+    @pl.when(me_t == 0)
+    def _():
+        xbuf[0:2] = jnp.zeros((2, rows + 2, cols, chans), BF16)
+
     frame_conv(1)
     frame_conv(0)
+    hear(2)
     for t in range(frames - 1, -1, -1):
         finish(t)
+
     out = dot(routes[...], lat[...].reshape(toks, width)) + extra[...]
     sides = [
         out[:, k * LANES : (k + 1) * LANES].reshape(owners, CAP, LANES)
         for k in range(width // LANES)
     ]
     pay[...] = jnp.concatenate(sides, axis=1).astype(BF16)
-    leave = pltpu.make_async_copy(pay, payload_out, out_sem.at[frames])
-    leave.start()
-    for copy in (late, to_up, to_down, early, corner_up, corner_down):
+    mine_copy = pltpu.make_async_copy(pay.at[me], arrived.at[me], out_sem.at[frames])
+    mine_copy.start()
+
+    def send(k, _):
+        to = lax.rem(me + k, owners)
+        pltpu.make_async_remote_copy(
+            src_ref=pay.at[to], dst_ref=arrived.at[me], send_sem=go_sem, recv_sem=come_sem,
+            device_id={"tm": to // nh, "height": lax.rem(to, nh)}, device_id_type=MESH,
+        ).start()
+        return 0
+
+    lax.fori_loop(1, owners, send, 0)
+    for copy in halos:
         copy.wait_send()
     for t in range(frames):
         for k in range(nh - 1):
             stat_copy(t, k).wait_send()
-        pltpu.make_async_copy(
-            lat.at[pl.ds(t * half_rows, half_rows)], latent_out.at[t], out_sem.at[t]
-        ).wait()
-    leave.wait()
+        latent_copy(t).wait()
+    mine_copy.wait()
+    others = pl.ds(0, owners - 1)
+    pltpu.make_async_copy(pay.at[others], arrived.at[others], come_sem).wait()
+    pltpu.make_async_copy(pay.at[others], arrived.at[others], go_sem).wait()
 
 
 def compact(arrived, owners, width):
@@ -296,8 +358,11 @@
     return dot(chosen, rows).astype(BF16)
 
 
-def compact_kernel(owners, width, arrived, routed):
+def compact_kernel(owners, width, arrived, latent_in, routed, latent_out, sem):
+    copy = pltpu.make_async_copy(latent_in, latent_out, sem)
+    copy.start()
     routed[...] = compact(arrived[...], owners, width)
+    copy.wait()
 
 
 def on_device(
@@ -309,20 +374,30 @@
     toks = frames * half_rows * half_cols
     owners = ntm * nh
     slots = owners * CAP
-    any_spec = pl.BlockSpec(memory_space=pl.ANY)
+    fast = 8 if ntm % 8 == 0 else ntm
+    hbm = pl.BlockSpec(memory_space=pltpu.HBM)
     vmem = pl.BlockSpec(memory_space=pltpu.VMEM)
     tiles = CAP * width // LANES
-    latent, payload = pl.pallas_call(
-        functools.partial(encode_kernel, ntm, nh, (frames, rows, cols, chans, width)),
-        out_shape=(
-            jax.ShapeDtypeStruct((frames, half_rows, half_cols, width), BF16),
-            jax.ShapeDtypeStruct((owners, tiles, LANES), BF16),
+    latent_shape = jax.ShapeDtypeStruct((frames, half_rows, half_cols, width), BF16)
+    dma = pltpu.SemaphoreType.DMA
+    latent, arrived = pl.pallas_call(
+        functools.partial(
+            encode_kernel, ntm, nh, (frames, rows, cols, chans, width), (fast, ntm // fast)
         ),
-        in_specs=[any_spec, any_spec] + [vmem] * 7,
-        out_specs=(any_spec, any_spec),
+        out_shape=(latent_shape, jax.ShapeDtypeStruct((owners, tiles, LANES), BF16)),
+        in_specs=[hbm] * 9,
+        out_specs=(hbm, hbm),
         scratch_shapes=[
             pltpu.VMEM((frames + 2, rows + 2, cols, chans), BF16),
-            pltpu.VMEM((9, chans, 3 * chans), BF16),
+            pltpu.VMEM((3, 3, chans, 2 * chans), BF16),
+            pltpu.VMEM((3, 4, chans, 2 * chans), BF16),
+            pltpu.VMEM((1, chans), F32),
+            pltpu.VMEM((1, chans), F32),
+            pltpu.VMEM(down_weight.shape, BF16),
+            pltpu.VMEM(length_table.shape, F32),
+            pltpu.VMEM(keep.shape, jnp.int32),
+            pltpu.VMEM(keep.shape, jnp.int32),
+            pltpu.VMEM(keep.shape, jnp.int32),
             pltpu.VMEM((frames, rows, cols, chans), F32),
             pltpu.VMEM((nh, frames, 16, chans), F32),
             pltpu.VMEM((2, frames * half_rows, LANES), F32),
@@ -330,13 +405,15 @@
             pltpu.VMEM((slots, width), F32),
             pltpu.VMEM((frames * half_rows, half_cols, width), BF16),
             pltpu.VMEM((owners, tiles, LANES), BF16),
-            pltpu.SemaphoreType.DMA,
-            pltpu.SemaphoreType.DMA((3,)),
-            pltpu.SemaphoreType.DMA((6,)),
-            pltpu.SemaphoreType.DMA((6,)),
-            pltpu.SemaphoreType.DMA((frames, nh - 1)),
-            pltpu.SemaphoreType.DMA((frames, nh)),
-            pltpu.SemaphoreType.DMA((frames + 1,)),
+            dma((12,)),
+            dma((6,)),
+            dma((6,)),
+            dma((frames, nh - 1)),
+            dma((frames, nh)),
+            pltpu.SemaphoreType.REGULAR((3,)),
+            dma((frames + 1,)),
+            dma,
+            dma,
         ],
         compiler_params=pltpu.CompilerParams(
             collective_id=0, has_side_effects=True, vmem_limit_bytes=48 * 1024 * 1024
@@ -344,7 +421,7 @@
         name="encode",
     )(
         video,
-        conv_weight.reshape(9, 3, chans, chans),
+        conv_weight,
         norm_gain.reshape(1, chans),
         norm_bias.reshape(1, chans),
         down_weight,
@@ -353,17 +430,15 @@
         run_length,
         owner,
     )
-    arrived = lax.all_to_all(
-        payload, ("tm", "height"), split_axis=0, concat_axis=0, tiled=True
-    )
-    routed = pl.pallas_call(
+    routed, latent = pl.pallas_call(
         functools.partial(compact_kernel, owners, width),
-        out_shape=jax.ShapeDtypeStruct((slots, width), BF16),
-        in_specs=[vmem],
-        out_specs=vmem,
+        out_shape=(jax.ShapeDtypeStruct((slots, width), BF16), latent_shape),
+        in_specs=[vmem, hbm],
+        out_specs=(vmem, hbm),
+        scratch_shapes=[dma],
         compiler_params=pltpu.CompilerParams(vmem_limit_bytes=48 * 1024 * 1024),
         name="compact",
-    )(arrived)
+    )(arrived, latent)
     return latent, routed
 
 

time: 61.6 us -> 47.1 us (0.76)
  waiting for transfers between devices: 13.8 us -> 0 us
  Pallas kernels: 28.6 us -> 38.5 us
  starting transfers between devices: 9.7 us -> 0 us
  local copies, waits for them, and re-layouts: 8.36 us -> 7.52 us
    all_to_all x1 -> x0, waiting for transfers between devices: 13.8 us -> none  [on_device(): lax.all_to_all(payload, ('tm', 'height'), split_axis=0, concat_axis=0, ti...]
    pallas_call x1, Pallas kernels: 26.9 us -> 36.7 us  [on_device(): pl.pallas_call(functools.partial(encode_kernel, ntm, nh, (frames, rows, c...]
    all_to_all x1 -> x0, starting transfers between devices: 9.7 us -> none  [on_device(): lax.all_to_all(payload, ('tm', 'height'), split_axis=0, concat_axis=0, ti...]
    unnamed x19 -> x18, local copies, waits for them, and re-layouts: 8.36 us -> 7.52 us
  transfers between devices with their start and end apart: 1 -> 0, of which waited for: 1 -> 0; matrix products, arithmetic and copies ran while one was open for 0% -> 0% of each run, Pallas kernels for 0% -> 0%
where the time goes in v2:
time: 47.1 us; the launch traced here: 46.7 us
  Pallas kernels  38.5 us (82%)
  local copies, waits for them, and re-layouts  7.52 us (16%)
  between operations  0.66 us (1%)
    pallas_call x1, Pallas kernels, on_device(): pl.pallas_call(functools.partial(encode_kernel, ntm, nh, (frames, rows, c...  36.7 us
    unnamed x18, local copies, waits for them, and re-layouts  7.52 us
    pallas_call x1, Pallas kernels, on_device(): pl.pallas_call(functools.partial(compact_kernel, owners, width), out_shap...  1.77 us

profile of v2, /device:TPU:1, one launch (start us, length us, event | category | flops | bytes accessed | tf_op | source)
XLA Modules:
  0.0 46.7 jit_solution(3438365093360493751)
XLA Ops:
  0.6 0.0 copy-start
  0.6 1.3 %copy-done = bf16[4,8,160,128]{3,2,1,0:T(8,128)(2,1)S(1)} copy-done((bf16[4,8,160,128]{3,2,1,0:T(8,128)(2,1)S(1)}, bf16[4,8,160,128]{3,2,1,0:T(8,128)(2,1)}, u32[]{:S(2)}) %copy-start) | copy-done | bytes 1310744
  2.0 0.0 copy-start.1
  2.0 1.2 %copy-done.1 = bf16[3,3,3,128,128]{4,3,2,1,0:T(8,128)(2,1)S(1)} copy-done((bf16[3,3,3,128,128]{4,3,2,1,0:T(8,128)(2,1)S(1)}, bf16[3,3,3,128,128]{4,3,2,1,0:T(8,128)(2,1)}, u32[]{:S(2)}) %copy-start.1) | copy-done | bytes 884760
  3.1 0.0 copy-start.2
  3.1 0.9 %copy-done.2 = bf16[512,256]{1,0:T(8,128)(2,1)S(1)} copy-done((bf16[512,256]{1,0:T(8,128)(2,1)S(1)}, bf16[512,256]{1,0:T(8,128)(2,1)}, u32[]{:S(2)}) %copy-start.2) | copy-done | bytes 262168
  4.1 0.0 copy-start.3
  4.1 0.7 %copy-done.3 = f32[8,256]{1,0:T(8,128)S(1)} copy-done((f32[8,256]{1,0:T(8,128)S(1)}, f32[8,256]{1,0:T(8,128)}, u32[]{:S(2)}) %copy-start.3) | copy-done | bytes 8216
  4.8 0.0 copy-start.4
  4.8 0.7 %copy-done.4 = s32[4,4,80]{2,1,0:T(4,128)S(1)} copy-done((s32[4,4,80]{2,1,0:T(4,128)S(1)}, s32[4,4,80]{2,1,0:T(4,128)}, u32[]{:S(2)}) %copy-start.4) | copy-done | bytes 5144
  5.5 0.0 copy-start.5
  5.5 0.7 %copy-done.5 = s32[4,4,80]{2,1,0:T(4,128)S(1)} copy-done((s32[4,4,80]{2,1,0:T(4,128)S(1)}, s32[4,4,80]{2,1,0:T(4,128)}, u32[]{:S(2)}) %copy-start.5) | copy-done | bytes 5144
  6.2 0.0 copy-start.6
  6.2 0.7 %copy-done.6 = s32[4,4,80]{2,1,0:T(4,128)S(1)} copy-done((s32[4,4,80]{2,1,0:T(4,128)S(1)}, s32[4,4,80]{2,1,0:T(4,128)}, u32[]{:S(2)}) %copy-start.6) | copy-done | bytes 5144
  6.9 0.0 copy-start.7
  6.9 0.7 %copy-done.7 = f32[128]{0:T(128)S(1)} copy-done((f32[128]{0:T(128)S(1)}, f32[128]{0:T(128)}, u32[]{:S(2)}) %copy-start.7) | copy-done | bytes 536
  7.5 0.0 copy-start.8
  7.5 0.7 %copy-done.8 = f32[128]{0:T(128)S(1)} copy-done((f32[128]{0:T(128)S(1)}, f32[128]{0:T(128)}, u32[]{:S(2)}) %copy-start.8) | copy-done | bytes 536
  8.2 36.7 %encode.1 = (bf16[4,4,80,256]{3,2,1,0:T(8,128)(2,1)S(1)}, bf16[128,16,128]{2,1,0:T(8,128)(2,1)S(1)}) custom-call(bf16[4,8,160,128]{3,2,1,0:T(8,128)(2,1)S(1)} %copy-done, bf16[3,3,3,128,128]{4,3,2,1,0:T(8,128)(2,1)S(1)} %copy-done.1, f32[1,128]{1,0:T(1,128)S(1)} %bitcast.2, f32[1,128]{1,0:T(1,128)S(1)} %bitcast.3, bf16[512,256]{1,0:T(8,128)(2,1)S(1)} %copy-done.2, ...), custom_call_target="tpu_custom_call" | custom-call | tf_op jit(solution)/shard_map/encode/pallas_call | solution.py:383
  44.9 1.8 %compact.1 = (bf16[1024,256]{1,0:T(8,128)(2,1)}, bf16[4,4,80,256]{3,2,1,0:T(8,128)(2,1)}) custom-call(bf16[128,16,128]{2,1,0:T(8,128)(2,1)S(1)} %get-tuple-element.6.arrived, bf16[4,4,80,256]{3,2,1,0:T(8,128)(2,1)S(1)} %get-tuple-element.7.latent_in), custom_call_target="tpu_custom_call" | custom-call | tf_op jit(solution)/shard_map/compact/pallas_call | solution.py:433
Async XLA Ops:
  0.6 1.3 %copy-start = (bf16[4,8,160,128]{3,2,1,0:T(8,128)(2,1)S(1)}, bf16[4,8,160,128]{3,2,1,0:T(8,128)(2,1)}, u32[]{:S(2)}) copy-start(bf16[4,8,160,128]{3,2,1,0:T(8,128)(2,1)} %video_in.1) | copy-start | bytes 3932164
  2.0 1.2 %copy-start.1 = (bf16[3,3,3,128,128]{4,3,2,1,0:T(8,128)(2,1)S(1)}, bf16[3,3,3,128,128]{4,3,2,1,0:T(8,128)(2,1)}, u32[]{:S(2)}) copy-start(bf16[3,3,3,128,128]{4,3,2,1,0:T(8,128)(2,1)} %weight_in.1) | copy-start | bytes 2654212
  3.1 0.9 %copy-start.2 = (bf16[512,256]{1,0:T(8,128)(2,1)S(1)}, bf16[512,256]{1,0:T(8,128)(2,1)}, u32[]{:S(2)}) copy-start(bf16[512,256]{1,0:T(8,128)(2,1)} %down_in.1) | copy-start | bytes 786436
  4.1 0.7 %copy-start.3 = (f32[8,256]{1,0:T(8,128)S(1)}, f32[8,256]{1,0:T(8,128)}, u32[]{:S(2)}) copy-start(f32[8,256]{1,0:T(8,128)} %table_in.1) | copy-start | bytes 24580
  4.8 0.7 %copy-start.4 = (s32[4,4,80]{2,1,0:T(4,128)S(1)}, s32[4,4,80]{2,1,0:T(4,128)}, u32[]{:S(2)}) copy-start(s32[4,4,80]{2,1,0:T(4,128)} %keep_in.1) | copy-start | bytes 15364
  5.5 0.7 %copy-start.5 = (s32[4,4,80]{2,1,0:T(4,128)S(1)}, s32[4,4,80]{2,1,0:T(4,128)}, u32[]{:S(2)}) copy-start(s32[4,4,80]{2,1,0:T(4,128)} %run_in.1) | copy-start | bytes 15364
  6.2 0.7 %copy-start.6 = (s32[4,4,80]{2,1,0:T(4,128)S(1)}, s32[4,4,80]{2,1,0:T(4,128)}, u32[]{:S(2)}) copy-start(s32[4,4,80]{2,1,0:T(4,128)} %owner_in.1) | copy-start | bytes 15364
  6.9 0.7 %copy-start.7 = (f32[128]{0:T(128)S(1)}, f32[128]{0:T(128)}, u32[]{:S(2)}) copy-start(f32[128]{0:T(128)} %param.11) | copy-start | bytes 1540
  7.5 0.7 %copy-start.8 = (f32[128]{0:T(128)S(1)}, f32[128]{0:T(128)}, u32[]{:S(2)}) copy-start(f32[128]{0:T(128)} %param.12) | copy-start | bytes 1540

commit v3 on v2

--- a/solution.py
+++ b/solution.py
@@ -47,7 +47,8 @@
 ):
     frames, rows, cols, chans, width = shapes
     half_rows, half_cols = rows // 2, cols // 2
-    toks = frames * half_rows * half_cols
+    patches = half_rows * half_cols
+    toks = frames * patches
     owners = ntm * nh
     slots = owners * CAP
     me_t, me_h = lax.axis_index("tm"), lax.axis_index("height")
@@ -63,7 +64,7 @@
         [(plane * fast + lax.rem(line + k, fast), me_h) for k in range(1, fast)],
         [(lax.rem(plane + k, slow) * fast + line, me_h) for k in range(1, slow)],
     ]
-    sources = [(last_t, me_h), (last_t, up), (last_t, down_h)]
+    sources = [(last_t, me_h)]
     sources += [target for group in rounds for target in group]
     barrier = pltpu.get_barrier_semaphore()
     for t, h in sources:
@@ -95,16 +96,18 @@
             device_id={"tm": t, "height": h}, device_id_type=MESH,
         )
 
-    own_rows = pl.ds(1, rows)
+    pair = pl.ds(frames - 2, 2)
+    inner = pl.ds(1, rows - 2)
     to_up = halo(0, video_in.at[:, 0], xbuf.at[pl.ds(2, frames), rows + 1], me_t, up)
     to_down = halo(1, video_in.at[:, rows - 1], xbuf.at[pl.ds(2, frames), 0], me_t, down_h)
-    late = halo(2, video_in.at[frames - 1], xbuf.at[1, own_rows], next_t, me_h)
-    early = halo(3, video_in.at[frames - 2], xbuf.at[0, own_rows], next_t, me_h)
-    pair = pl.ds(frames - 2, 2)
-    corner_up = halo(4, video_in.at[pair, 0], xbuf.at[pl.ds(0, 2), rows + 1], next_t, up)
-    corner_down = halo(5, video_in.at[pair, rows - 1], xbuf.at[pl.ds(0, 2), 0], next_t, down_h)
-    halos = (late, to_up, to_down, early, corner_up, corner_down)
-    for copy in halos:
+    top = halo(2, video_in.at[pair, 0], xbuf.at[pl.ds(0, 2), 1], next_t, me_h)
+    bottom = halo(3, video_in.at[pair, rows - 1], xbuf.at[pl.ds(0, 2), rows], next_t, me_h)
+    late = halo(4, video_in.at[frames - 1, inner], xbuf.at[1, pl.ds(2, rows - 2)], next_t, me_h)
+    early = halo(5, video_in.at[frames - 2, inner], xbuf.at[0, pl.ds(2, rows - 2)], next_t, me_h)
+    corner_up = halo(6, xbuf.at[pl.ds(0, 2), 1], xbuf.at[pl.ds(0, 2), rows + 1], me_t, up)
+    corner_down = halo(7, xbuf.at[pl.ds(0, 2), rows], xbuf.at[pl.ds(0, 2), 0], me_t, down_h)
+    halos = (top, bottom, to_up, to_down, late, early, corner_up, corner_down)
+    for copy in halos[:6]:
         copy.start()
 
     def tell(k):
@@ -148,7 +151,8 @@
         ahead = dot(block.astype(BF16), before_lane) + carry
         carry = carry + jnp.sum(block, axis=1, keepdims=True)
         rank = jnp.sum(ahead * block, axis=0, keepdims=True).astype(jnp.int32)
-        slot = jnp.where(code_i[:, at] < owners, code_i[:, at] * CAP + rank, -1)
+        place = lax.rem(code_i[:, at] + (owners - me), owners)
+        slot = jnp.where(code_i[:, at] < owners, place * CAP + rank, -1)
         routes[:, at] = onehot(iota((slots, LANES), 0) == slot)
     lanes_t = 4 * LMAX
     row_of = iota((lanes_t, toks), 0)
@@ -169,46 +173,55 @@
         copy.wait()
     hear(0)
     tell(1)
+    top.wait_recv()
+    corner_up.start()
+    bottom.wait_recv()
+    corner_down.start()
 
     first = iota((1, cols, chans), 1) == 0
     final = iota((1, cols, chans), 1) == cols - 1
 
-    def convolve(t, r0, count):
-        half = count // 2
+    def gather(lines, a, b):
+        return jnp.concatenate([xbuf[t + a, r + b] for t, r in lines], axis=0)
+
+    def convolve(lines, paired, fresh):
+        count = len(lines)
         window = jnp.concatenate(
-            [
-                xbuf[t + a, pl.ds(r0 + b, count)].reshape(count * cols, chans)
-                for a in range(3)
-                for b in range(3)
-            ],
-            axis=1,
+            [gather(lines, a, b) for a in range(3) for b in range(3)], axis=1
         )
         taps = dot(window, wpair[...].reshape(9 * chans, 2 * chans))
         left = pltpu.roll(taps[:, :chans], 1, 0).reshape(count, cols, chans)
         out = taps[:, chans:].reshape(count, cols, chans) + jnp.where(first, 0.0, left)
-        window = jnp.concatenate(
-            [
-                jnp.concatenate([xbuf[t + a, r0 + b + 2 * i] for i in range(half)], axis=0)
-                for a in range(3)
-                for b in range(4)
-            ],
-            axis=1,
-        )
-        taps = dot(window, wlast[...].reshape(12 * chans, 2 * chans))
-        right = jnp.concatenate(
-            [
-                pltpu.roll(taps[:, k * chans : (k + 1) * chans], half * cols - 1, 0).reshape(
-                    half, 1, cols, chans
-                )
-                for k in range(2)
-            ],
-            axis=1,
-        ).reshape(count, cols, chans)
-        out = out + jnp.where(final, 0.0, right)
-        hidden[t, pl.ds(r0, count)] = out
-        tiles = out.reshape(count * cols // 8, 8, chans)
-        stat[me_h, t, pl.ds(0, 8)] = jnp.sum(tiles, axis=0)
-        stat[me_h, t, pl.ds(8, 8)] = jnp.sum(tiles * tiles, axis=0)
+        if paired:
+            half = count // 2
+            window = jnp.concatenate(
+                [gather(lines[::2], a, b) for a in range(3) for b in range(4)], axis=1
+            )
+            taps = dot(window, wlast[...].reshape(12 * chans, 2 * chans))
+            right = jnp.concatenate(
+                [
+                    pltpu.roll(
+                        taps[:, k * chans : (k + 1) * chans], half * cols - 1, 0
+                    ).reshape(half, 1, cols, chans)
+                    for k in range(2)
+                ],
+                axis=1,
+            )
+        else:
+            taps = dot(window, wlast[:, 0:3, :, 0:chans].reshape(9 * chans, chans))
+            right = pltpu.roll(taps, count * cols - 1, 0)
+        out = out + jnp.where(final, 0.0, right.reshape(count, cols, chans))
+        for t in sorted({t for t, _ in lines}):
+            mine = [k for k, line in enumerate(lines) if line[0] == t]
+            for k in mine:
+                hidden[t, lines[k][1]] = out[k]
+            tiles = out[mine[0] : mine[-1] + 1].reshape(len(mine) * cols // 8, 8, chans)
+            total, square = jnp.sum(tiles, axis=0), jnp.sum(tiles * tiles, axis=0)
+            if not fresh:
+                total = total + stat[me_h, t, pl.ds(0, 8)]
+                square = square + stat[me_h, t, pl.ds(8, 8)]
+            stat[me_h, t, pl.ds(0, 8)] = total
+            stat[me_h, t, pl.ds(8, 8)] = square
 
     def clear_rows(at, count):
         @pl.when(me_h == 0)
@@ -233,8 +246,7 @@
             device_id={"tm": me_t, "height": peers[k]}, device_id_type=MESH,
         )
 
-    def frame_conv(t):
-        convolve(t, 0, rows)
+    def send_stat(t):
         for k in range(nh - 1):
             stat_copy(t, k).start()
 
@@ -271,58 +283,84 @@
             ],
             axis=0,
         )
-        lat[pl.ds(t * half_rows, half_rows)] = (
-            dot(merged, down[...]).astype(BF16).reshape(half_rows, half_cols, width)
-        )
+        lat[pl.ds(t * patches, patches)] = dot(merged, down[...]).astype(BF16)
         latent_copy(t).start()
 
     def latent_copy(t):
         return pltpu.make_async_copy(
-            lat.at[pl.ds(t * half_rows, half_rows)], latent_out.at[t], out_sem.at[t]
-        )
-
+            lat.at[pl.ds(t * patches, patches)], latent_out.at[t], out_sem.at[t]
+        )
+
+    for t in range(frames - 1, 1, -1):
+        convolve([(t, r) for r in range(1, rows - 1)], True, True)
     to_up.wait_recv()
     to_down.wait_recv()
     clear_rows(2, frames)
+    convolve([(t, r) for t in range(2, frames) for r in (0, rows - 1)], False, False)
     for t in range(frames - 1, 1, -1):
-        frame_conv(t)
+        send_stat(t)
     hear(1)
     tell(2)
     late.wait_recv()
     corner_up.wait_recv()
     corner_down.wait_recv()
-    early.wait_recv()
+    corner_up.wait_send()
+    corner_down.wait_send()
     clear_rows(0, 2)
 
     @pl.when(me_t == 0)
     def _():
-        xbuf[0:2] = jnp.zeros((2, rows + 2, cols, chans), BF16)
-
-    frame_conv(1)
-    frame_conv(0)
+        xbuf[1] = jnp.zeros((rows + 2, cols, chans), BF16)
+
+    convolve([(1, r) for r in range(rows)], True, True)
+    send_stat(1)
+    early.wait_recv()
+
+    @pl.when(me_t == 0)
+    def _():
+        xbuf[0] = jnp.zeros((rows + 2, cols, chans), BF16)
+
+    convolve([(0, r) for r in range(rows)], True, True)
+    send_stat(0)
     hear(2)
-    for t in range(frames - 1, -1, -1):
+    for t in range(frames - 1, 0, -1):
         finish(t)
-
-    out = dot(routes[...], lat[...].reshape(toks, width)) + extra[...]
-    sides = [
-        out[:, k * LANES : (k + 1) * LANES].reshape(owners, CAP, LANES)
-        for k in range(width // LANES)
-    ]
-    pay[...] = jnp.concatenate(sides, axis=1).astype(BF16)
-    mine_copy = pltpu.make_async_copy(pay.at[me], arrived.at[me], out_sem.at[frames])
+    done = -(-patches // LANES) * LANES
+    extra[...] += dot(routes[:, done:], lat[pl.ds(done, toks - done)])
+    finish(0)
+    batch = min(16, owners)
+
+    def leave(i, _):
+        at = pl.multiple_of(i * (batch * CAP), batch * CAP)
+        here = pl.ds(at, batch * CAP)
+        out = dot(routes[here, pl.ds(0, done)], lat[pl.ds(0, done)]) + extra[here]
+        sides = [
+            out[:, k * LANES : (k + 1) * LANES].reshape(batch, CAP, LANES)
+            for k in range(width // LANES)
+        ]
+        pay[pl.ds(i * batch, batch)] = jnp.concatenate(sides, axis=1).astype(BF16)
+        for j in range(batch):
+            k = i * batch + j
+            to = lax.rem(me + k, owners)
+
+            def send():
+                pltpu.make_async_remote_copy(
+                    src_ref=pay.at[k], dst_ref=arrived.at[me],
+                    send_sem=go_sem, recv_sem=come_sem,
+                    device_id={"tm": to // nh, "height": lax.rem(to, nh)},
+                    device_id_type=MESH,
+                ).start()
+
+            if j:
+                send()
+            else:
+                pl.when(k > 0)(send)
+        return 0
+
+    lax.fori_loop(0, owners // batch, leave, 0)
+    mine_copy = pltpu.make_async_copy(pay.at[0], arrived.at[me], out_sem.at[frames])
     mine_copy.start()
-
-    def send(k, _):
-        to = lax.rem(me + k, owners)
-        pltpu.make_async_remote_copy(
-            src_ref=pay.at[to], dst_ref=arrived.at[me], send_sem=go_sem, recv_sem=come_sem,
-            device_id={"tm": to // nh, "height": lax.rem(to, nh)}, device_id_type=MESH,
-        ).start()
-        return 0
-
-    lax.fori_loop(1, owners, send, 0)
-    for copy in halos:
+    for copy in halos[:6]:
         copy.wait_send()
     for t in range(frames):
         for k in range(nh - 1):
@@ -378,8 +416,19 @@
     hbm = pl.BlockSpec(memory_space=pltpu.HBM)
     vmem = pl.BlockSpec(memory_space=pltpu.VMEM)
     tiles = CAP * width // LANES
-    latent_shape = jax.ShapeDtypeStruct((frames, half_rows, half_cols, width), BF16)
+    latent_shape = jax.ShapeDtypeStruct((frames, half_rows * half_cols, width), BF16)
     dma = pltpu.SemaphoreType.DMA
+    operands = (
+        video,
+        conv_weight,
+        norm_gain.reshape(1, chans),
+        norm_bias.reshape(1, chans),
+        down_weight,
+        length_table,
+        keep,
+        run_length,
+        owner,
+    )
     latent, arrived = pl.pallas_call(
         functools.partial(
             encode_kernel, ntm, nh, (frames, rows, cols, chans, width), (fast, ntm // fast)
@@ -403,11 +452,11 @@
             pltpu.VMEM((2, frames * half_rows, LANES), F32),
             pltpu.VMEM((slots, toks), BF16),
             pltpu.VMEM((slots, width), F32),
-            pltpu.VMEM((frames * half_rows, half_cols, width), BF16),
+            pltpu.VMEM((toks, width), BF16),
             pltpu.VMEM((owners, tiles, LANES), BF16),
             dma((12,)),
-            dma((6,)),
-            dma((6,)),
+            dma((8,)),
+            dma((8,)),
             dma((frames, nh - 1)),
             dma((frames, nh)),
             pltpu.SemaphoreType.REGULAR((3,)),
@@ -419,17 +468,7 @@
             collective_id=0, has_side_effects=True, vmem_limit_bytes=48 * 1024 * 1024
         ),
         name="encode",
-    )(
-        video,
-        conv_weight,
-        norm_gain.reshape(1, chans),
-        norm_bias.reshape(1, chans),
-        down_weight,
-        length_table,
-        keep,
-        run_length,
-        owner,
-    )
+    )(*(pltpu.with_memory_space_constraint(array, pltpu.HBM) for array in operands))
     routed, latent = pl.pallas_call(
         functools.partial(compact_kernel, owners, width),
         out_shape=(jax.ShapeDtypeStruct((slots, width), BF16), latent_shape),
@@ -439,7 +478,7 @@
         compiler_params=pltpu.CompilerParams(vmem_limit_bytes=48 * 1024 * 1024),
         name="compact",
     )(arrived, latent)
-    return latent, routed
+    return latent.reshape(frames, half_rows, half_cols, width), routed
 
 
 def solution(mesh):

time: 47.1 us -> 35 us (0.74)
  local copies, waits for them, and re-layouts: 7.52 us -> 0 us
  Pallas kernels: 38.5 us -> 34.3 us
    unnamed x18 -> x0, local copies, waits for them, and re-layouts: 7.52 us -> none
    pallas_call x1, Pallas kernels: 36.7 us -> 32.5 us  [on_device(): pl.pallas_call(functools.partial(encode_kernel, ntm, nh, (frames, rows, c...]
where the time goes in v3:
time: 35 us; the launch traced here: 34.9 us
  Pallas kernels  34.3 us (98%)
  between operations  0.64 us (2%)
    pallas_call x1, Pallas kernels, on_device(): pl.pallas_call(functools.partial(encode_kernel, ntm, nh, (frames, rows, c...  32.5 us
    pallas_call x1, Pallas kernels, on_device(): pl.pallas_call(functools.partial(compact_kernel, owners, width), out_shap...  1.77 us

profile of v3, /device:TPU:1, one launch (start us, length us, event | category | flops | bytes accessed | tf_op | source)
XLA Modules:
  0.0 34.9 jit_solution(2565896327228009279)
XLA Ops:
  0.6 32.5 %encode.1 = (bf16[4,320,256]{2,1,0:T(8,128)(2,1)S(1)}, bf16[128,16,128]{2,1,0:T(8,128)(2,1)S(1)}) custom-call(bf16[4,8,160,128]{3,2,1,0:T(8,128)(2,1)} %video_in.1, bf16[3,3,3,128,128]{4,3,2,1,0:T(8,128)(2,1)} %weight_in.1, f32[1,128]{1,0:T(1,128)} %bitcast.3, f32[1,128]{1,0:T(1,128)} %bitcast.4, bf16[512,256]{1,0:T(8,128)(2,1)} %down_in.1, ...), custom_call_target="tpu_custom_call" | custom-call | tf_op jit(solution)/shard_map/encode/pallas_call | solution.py:432
  33.1 1.8 %compact.1 = (bf16[1024,256]{1,0:T(8,128)(2,1)}, bf16[4,320,256]{2,1,0:T(8,128)(2,1)}) custom-call(bf16[128,16,128]{2,1,0:T(8,128)(2,1)S(1)} %get-tuple-element.6.arrived, bf16[4,320,256]{2,1,0:T(8,128)(2,1)S(1)} %get-tuple-element.7.latent_in), custom_call_target="tpu_custom_call" | custom-call | tf_op jit(solution)/shard_map/compact/pallas_call | solution.py:472

commit v4 on v3

v4 whole, which is shorter than its diff:
```python
import functools
import itertools

import jax
import jax.numpy as jnp
from jax import lax
from jax.experimental import pallas as pl
from jax.experimental.pallas import tpu as pltpu
from jax.sharding import PartitionSpec as P

GROUPS = 32
LMAX = 8
CAP = 8
EPSILON = 1e-06
LANES = 128
TURNS = ((3, 2, 1, 0), (2, 3, 1, 0), (2, 3, 1, 0), (1, 0))
EMPTY = 2.0**127
LIMIT = 2.0**126
MESH = pl.DeviceIdType.MESH
F32 = jnp.float32
BF16 = jnp.bfloat16


def dot(a, b):
    return jnp.dot(a, b, preferred_element_type=F32)


def dot_t(a, b, precision=None):
    return lax.dot_general(
        a, b, (((1,), (1,)), ((), ())), preferred_element_type=F32, precision=precision
    )


def iota(shape, dim):
    return lax.broadcasted_iota(jnp.int32, shape, dim)


def onehot(mask):
    return jnp.where(mask, 1.0, 0.0).astype(BF16)


def heights(patches, frames):
    head = (patches // LANES + 1) * LANES
    return head, head + -(-(frames - 1) * patches // LANES) * LANES


def encode_kernel(
    ntm, nh, shapes, ways,
    video_in, weight_in, gain_in, bias_in, down_in, table_in, keep_in, run_in, owner_in,
    latent_out, arrived,
    xbuf, wpair, wlast, gain, bias, down, table, keep, run, owner,
    hidden, stat, routes, extra, lat, total, pay,
    in_sem, halo_send, halo_recv, stat_send, stat_recv, ready, out_sem, go_sem, come_sem,
):
    frames, rows, cols, chans, width = shapes
    half_rows, half_cols = rows // 2, cols // 2
    patches = half_rows * half_cols
    toks = frames * patches
    owners = ntm * nh
    slots = owners * CAP
    head, taken = heights(patches, frames)
    me_t, me_h = lax.axis_index("tm"), lax.axis_index("height")
    me = me_t * nh + me_h
    next_t, last_t = lax.rem(me_t + 1, ntm), lax.rem(me_t + ntm - 1, ntm)
    up, down_h = lax.rem(me_h + nh - 1, nh), lax.rem(me_h + 1, nh)
    peers = [lax.rem(me_h + k, nh) for k in range(1, nh)]

    rows_x, planes = ways
    assert owners == 2 * nh * rows_x * planes and all(n & (n - 1) == 0 for n in (nh, *ways))

    even = lax.rem(me_t, 2) == 0
    has_next, has_last = me_t < ntm - 1, me_t > 0

    def signal(semaphore, t, h):
        pl.semaphore_signal(
            semaphore, inc=1, device_id={"tm": t, "height": h}, device_id_type=MESH
        )

    across = [
        [(me_t, h) for h in peers],
        [(me_t ^ (2 * k), me_h) for k in range(1, rows_x)],
        [(me_t ^ (2 * rows_x * k), me_h) for k in range(1, planes)],
    ]
    barrier = pltpu.get_barrier_semaphore()

    @pl.when(has_last)
    def _():
        signal(barrier, last_t, me_h)

    for t, h in across[0]:
        signal(barrier, t, h)

    @pl.when(even)
    def _():
        for t, h in across[1] + across[2]:
            signal(barrier, t, h)

    loads = [
        (keep_in, keep), (run_in, run), (owner_in, owner), (table_in, table),
        (video_in, xbuf.at[pl.ds(2, frames), pl.ds(1, rows)]),
        (weight_in.at[:, :, 0], wpair.at[:, :, :, pl.ds(0, chans)]),
        (weight_in.at[:, :, 1], wpair.at[:, :, :, pl.ds(chans, chans)]),
        (weight_in.at[:, :, 2], wlast.at[:, pl.ds(0, 3), :, pl.ds(0, chans)]),
        (weight_in.at[:, :, 2], wlast.at[:, pl.ds(1, 3), :, pl.ds(chans, chans)]),
        (down_in, down), (gain_in, gain), (bias_in, bias),
    ]
    loads = [
        pltpu.make_async_copy(src, dst, in_sem.at[k]) for k, (src, dst) in enumerate(loads)
    ]
    for copy in loads:
        copy.start()
    wlast[:, 3, :, pl.ds(0, chans)] = jnp.zeros((3, chans, chans), BF16)
    wlast[:, 0, :, pl.ds(chans, chans)] = jnp.zeros((3, chans, chans), BF16)
    awaited = nh - 1 + jnp.where(has_next, 1, 0)
    pl.semaphore_wait(barrier, awaited + jnp.where(even, rows_x + planes - 2, 0))

    def halo(k, src, dst, t, h):
        return pltpu.make_async_remote_copy(
            src_ref=src, dst_ref=dst, send_sem=halo_send.at[k], recv_sem=halo_recv.at[k],
            device_id={"tm": t, "height": h}, device_id_type=MESH,
        )

    pair = pl.ds(frames - 2, 2)
    inner = pl.ds(1, rows - 2)
    to_up = halo(0, video_in.at[:, 0], xbuf.at[pl.ds(2, frames), rows + 1], me_t, up)
    to_down = halo(1, video_in.at[:, rows - 1], xbuf.at[pl.ds(2, frames), 0], me_t, down_h)
    top = halo(2, video_in.at[pair, 0], xbuf.at[pl.ds(0, 2), 1], next_t, me_h)
    bottom = halo(3, video_in.at[pair, rows - 1], xbuf.at[pl.ds(0, 2), rows], next_t, me_h)
    late = halo(4, video_in.at[frames - 1, inner], xbuf.at[1, pl.ds(2, rows - 2)], next_t, me_h)
    early = halo(5, video_in.at[frames - 2, inner], xbuf.at[0, pl.ds(2, rows - 2)], next_t, me_h)
    corner_up = halo(6, xbuf.at[pl.ds(0, 2), 1], xbuf.at[pl.ds(0, 2), rows + 1], me_t, up)
    corner_down = halo(7, xbuf.at[pl.ds(0, 2), rows], xbuf.at[pl.ds(0, 2), 0], me_t, down_h)
    onward = (top, bottom, late, early)

    @pl.when(has_next)
    def _():
        for copy in onward[:2]:
            copy.start()

    to_up.start()
    to_down.start()

    @pl.when(has_next)
    def _():
        for copy in onward[2:]:
            copy.start()

    def tell(k):
        @pl.when(even)
        def _():
            for t, h in across[k] if k < 3 else [(next_t, me_h)]:
                signal(ready.at[k], t, h)

    def hear(k):
        if k == 3 or across[k]:

            @pl.when(even if k < 3 else jnp.logical_not(even))
            def _():
                pl.semaphore_wait(ready.at[k], len(across[k]) if k < 3 else 1)

    tell(0)
    for copy in loads[:4]:
        copy.wait()
    def along(pieces, filler):
        row = [pieces[r] for r in range(half_rows)]
        row += [jnp.full((1, head - patches), filler, jnp.int32)]
        row += [pieces[r] for r in range(half_rows, frames * half_rows)]
        row += [jnp.full((1, taken - head - (toks - patches)), filler, jnp.int32)]
        return jnp.concatenate([piece for piece in row if piece.shape[1]], axis=1)

    lines = [(t, slice(r, r + 1)) for t in range(frames) for r in range(half_rows)]
    place = []
    for t, r in lines:
        place.append(jnp.where(keep[t, r] == 1, owner[t, r] ^ me, -1))
    place = along(place, -1)
    length = along([run[t, r] - 1 for t, r in lines], -1)
    member = iota((owners, taken), 0) == place
    before_lane = onehot(iota((LANES, LANES), 0) < iota((LANES, LANES), 1))
    kept = jnp.zeros((owners, 1), F32)
    for k in range(taken // LANES):
        at = slice(k * LANES, (k + 1) * LANES)
        block = jnp.where(member[:, at], 1.0, 0.0)
        ahead = dot(block.astype(BF16), before_lane) + kept
        kept = kept + jnp.sum(block, axis=1, keepdims=True)
        rank = jnp.sum(ahead * block, axis=0, keepdims=True).astype(jnp.int32)
        slot = jnp.where(place[:, at] < 0, -1, place[:, at] * CAP + rank)
        chosen = iota((slots, LANES), 0) == slot
        if k == patches // LANES:
            partly = chosen
        else:
            routes[:, at] = onehot(chosen)
    at = slice(patches // LANES * LANES, (patches // LANES + 1) * LANES)
    unused = iota((owners, CAP, LANES), 1).astype(F32) >= kept.reshape(owners, 1, 1)
    mark = unused & (iota((owners, CAP, LANES), 2) == patches % LANES)
    routes[:, at] = jnp.maximum(
        onehot(partly).astype(F32), jnp.where(mark, 1.0, 0.0).reshape(slots, LANES)
    ).astype(BF16)
    lat[pl.ds(patches, head - patches)] = jnp.where(
        iota((head - patches, width), 0) == 0, EMPTY, 0.0
    ).astype(BF16)
    if taken > head + toks - patches:
        tail = taken - head - (toks - patches)
        lat[pl.ds(taken - tail, tail)] = jnp.zeros((tail, width), BF16)
    row_of = iota((4 * LMAX, taken), 0)
    which = (lax.rem(row_of, LMAX) == length) & (row_of < 3 * LMAX)
    which = jnp.where(which, 1.0, 0.0).T.astype(BF16)
    part0 = table[...].astype(BF16)
    rest = table[...] - part0.astype(F32)
    part1 = rest.astype(BF16)
    part2 = (rest - part1.astype(F32)).astype(BF16)
    parts = jnp.concatenate(
        [part0.astype(F32), part1.astype(F32), part2.astype(F32), jnp.zeros((LMAX, width), F32)],
        axis=0,
    ).astype(BF16)
    extra[...] = dot(which, parts)

    for copy in loads[4:]:
        copy.wait()
    hear(0)
    tell(1)

    first = iota((1, 8, chans), 1) == 0
    final = iota((1, 8, chans), 1) == 7

    def gather(lines, a, b):
        return jnp.concatenate([xbuf[t + a, r + b] for t, r in lines], axis=0)

    def convolve(lines, paired, afters=(0, 1, 2)):
        count = len(lines)
        window = jnp.concatenate(
            [gather(lines, a, b) for a in afters for b in range(3)], axis=1
        )
        used = slice(afters[0], afters[-1] + 1)
        taps = dot(window, wpair[used].reshape(-1, 2 * chans))
        left = pltpu.roll(taps[:, :chans], 1, 0).reshape(count, cols, chans)
        left = jnp.concatenate([jnp.where(first, 0.0, left[:, :8]), left[:, 8:]], axis=1)
        out = taps[:, chans:].reshape(count, cols, chans) + left
        if paired:
            half = count // 2
            window = jnp.concatenate(
                [gather(lines[::2], a, b) for a in afters for b in range(4)], axis=1
            )
            taps = dot(window, wlast[used].reshape(-1, 2 * chans))
            right = jnp.concatenate(
                [
                    pltpu.roll(
                        taps[:, k * chans : (k + 1) * chans], half * cols - 1, 0
                    ).reshape(half, 1, cols, chans)
                    for k in range(2)
                ],
                axis=1,
            )
        else:
            taps = dot(window, wlast[used, 0:3, :, 0:chans].reshape(-1, chans))
            right = pltpu.roll(taps, count * cols - 1, 0)
        right = right.reshape(count, cols, chans)
        out = out + jnp.concatenate(
            [right[:, :-8], jnp.where(final, 0.0, right[:, -8:])], axis=1
        )
        for t in sorted({t for t, _ in lines}):
            mine = [k for k, line in enumerate(lines) if line[0] == t]
            if afters == (0,):
                out = out + hidden[t]
            for k in mine:
                hidden[t, lines[k][1]] = out[k]
            if afters == (1, 2):
                continue
            tiles = out[mine[0] : mine[-1] + 1].reshape(len(mine) * cols // 8, 8, chans)
            total, square = jnp.sum(tiles, axis=0), jnp.sum(tiles * tiles, axis=0)
            if not paired:
                total = total + stat[me_h, t, pl.ds(0, 8)]
                square = square + stat[me_h, t, pl.ds(8, 8)]
            stat[me_h, t, pl.ds(0, 8)] = total
            stat[me_h, t, pl.ds(8, 8)] = square

    def clear_rows(at, count):
        @pl.when(me_h == 0)
        def _():
            xbuf[pl.ds(at, count), 0] = jnp.zeros((count, cols, chans), BF16)

        @pl.when(me_h == nh - 1)
        def _():
            xbuf[pl.ds(at, count), rows + 1] = jnp.zeros((count, cols, chans), BF16)

    def stat_copy(t, k):
        return pltpu.make_async_remote_copy(
            src_ref=stat.at[me_h, t], dst_ref=stat.at[me_h, t],
            send_sem=stat_send.at[t, k], recv_sem=stat_recv.at[t, me_h],
            device_id={"tm": me_t, "height": peers[k]}, device_id_type=MESH,
        )

    def stat_arrival(t, k):
        return pltpu.make_async_remote_copy(
            src_ref=stat.at[peers[k], t], dst_ref=stat.at[peers[k], t],
            send_sem=stat_send.at[t, k], recv_sem=stat_recv.at[t, peers[k]],
            device_id={"tm": me_t, "height": peers[k]}, device_id_type=MESH,
        )

    def send_stat(t):
        for k in range(nh - 1):
            stat_copy(t, k).start()

    group_of = chans // GROUPS
    same = onehot(iota((chans, chans), 0) // group_of == iota((chans, chans), 1) // group_of)
    count = rows * nh * cols * group_of

    def finish(times):
        for t in times:
            for k in range(nh - 1):
                stat_arrival(t, k).wait_recv()
        sums = [
            jnp.sum(jnp.sum(stat[:, t], axis=0).reshape(2, 8, chans), axis=1) for t in times
        ]
        sums = jnp.concatenate(sums + [jnp.zeros((8 - 2 * len(times), chans), F32)], axis=0)
        part0 = sums.astype(BF16).astype(F32)
        part1 = (sums - part0).astype(BF16).astype(F32)
        parts = jnp.concatenate([part0, part1, sums - part0 - part1], axis=0).astype(BF16)
        grouped = dot(parts, same)
        grouped = (grouped[0:8] + grouped[8:16] + grouped[16:24]) / count
        for k, t in enumerate(times):
            average, squares = grouped[2 * k : 2 * k + 1], grouped[2 * k + 1 : 2 * k + 2]
            spread = squares - average * average
            finish_frame(t, average, 0.5 * (lax.rsqrt(spread + EPSILON) * gain[...]))

    def finish_frame(t, average, scale):
        shift = 0.5 * bias[...]

        def act(r, b):
            h = hidden[t, r, pl.ds(b, half_cols, stride=2), :]
            v = (h - average) * scale + shift
            return (v + v * jnp.tanh(v)).astype(BF16)

        merged = jnp.concatenate(
            [
                jnp.concatenate(
                    [act(2 * i + a, b) for a in range(2) for b in range(2)], axis=1
                )
                for i in range(half_rows)
            ],
            axis=0,
        )
        latent = dot(merged, down[...]).astype(BF16)
        latent_out[t] = latent
        at = pl.ds(0 if t == 0 else head + (t - 1) * patches, patches)
        lat[at] = (latent.astype(F32) + extra[at]).astype(BF16)

    interior, edges = range(1, rows - 1), (0, rows - 1)
    for t in range(frames - 1, 1, -1):
        convolve([(t, r) for r in interior], True)

    @pl.when(has_last)
    def _():
        top.wait_recv()
        corner_up.start()
        bottom.wait_recv()
        corner_down.start()

    hear(1)
    tell(2)
    to_up.wait_recv()
    to_down.wait_recv()
    clear_rows(2, frames)
    convolve([(t, r) for t in range(2, frames) for r in edges], False)
    for t in range(frames - 1, 1, -1):
        send_stat(t)

    @pl.when(has_last)
    def _():
        late.wait_recv()

    @pl.when(jnp.logical_not(has_last))
    def _():
        xbuf[0:2] = jnp.zeros((2, rows + 2, cols, chans), BF16)

    convolve([(1, r) for r in interior], True)
    convolve([(0, r) for r in interior], True, (1, 2))

    @pl.when(has_last)
    def _():
        corner_up.wait_recv()
        corner_down.wait_recv()

    clear_rows(0, 2)
    convolve([(1, r) for r in edges], False)
    send_stat(1)
    convolve([(0, r) for r in edges], False, (1, 2))

    @pl.when(has_last)
    def _():
        early.wait_recv()

    convolve([(0, r) for r in range(rows)], True, (0,))
    send_stat(0)
    hear(2)
    tell(3)
    finish(range(frames - 1, 0, -1))
    rest = pl.ds(head, taken - head)
    total[...] = dot(routes[:, rest], lat[rest])
    finish([0])
    hear(3)
    batch = owners // planes
    turns = [[k for k in order if k < n] for order, n in zip(TURNS, (planes, rows_x, nh, 2))]
    for z in turns[0]:
        here = pl.ds(z * batch * CAP, batch * CAP)
        out = dot(routes[here, pl.ds(0, head)], lat[pl.ds(0, head)]) + total[here]
        sides = [
            out[:, k * LANES : (k + 1) * LANES].reshape(batch, CAP, LANES)
            for k in range(width // LANES)
        ]
        pay[pl.ds(z * batch, batch)] = jnp.concatenate(sides, axis=1).astype(BF16)
        for x, h, core in itertools.product(*turns[1:]):
            t = (z * rows_x + x) * 2 + core
            k = t * nh + h
            if k:
                pltpu.make_async_remote_copy(
                    src_ref=pay.at[k], dst_ref=arrived.at[me],
                    send_sem=go_sem, recv_sem=come_sem,
                    device_id={"tm": me_t ^ t, "height": me_h ^ h}, device_id_type=MESH,
                ).start()
    mine_copy = pltpu.make_async_copy(pay.at[0], arrived.at[me], out_sem)
    mine_copy.start()

    @pl.when(has_next)
    def _():
        for copy in onward:
            copy.wait_send()

    @pl.when(has_last)
    def _():
        corner_up.wait_send()
        corner_down.wait_send()

    to_up.wait_send()
    to_down.wait_send()
    for t in range(frames):
        for k in range(nh - 1):
            stat_copy(t, k).wait_send()
    mine_copy.wait()
    others = pl.ds(0, owners - 1)
    pltpu.make_async_copy(pay.at[others], arrived.at[others], come_sem).wait()
    pltpu.make_async_copy(pay.at[others], arrived.at[others], go_sem).wait()


def compact(arrived, owners, width):
    slots = owners * CAP
    block = min(LANES, slots)
    tall = arrived.astype(F32)
    sides = [
        tall[:, k * CAP : (k + 1) * CAP].reshape(slots, LANES) for k in range(width // LANES)
    ]
    rows = jnp.concatenate(sides, axis=1).astype(BF16)
    pick = onehot(iota((8, LANES), 1) == 0)
    lead = dot_t(pick, sides[0].astype(BF16))
    ahead_of = onehot(iota((block, block), 0) < iota((block, block), 1))
    carry = jnp.zeros((8, 1), F32)
    places = []
    for k in range(slots // block):
        valid = jnp.where(lead[:, k * block : (k + 1) * block] < LIMIT, 1.0, 0.0)
        place = dot(valid.astype(BF16), ahead_of) + carry
        carry = carry + jnp.sum(valid, axis=1, keepdims=True)
        places.append(jnp.where(valid > 0.5, place, -1.0)[0:1].astype(jnp.int32))
    chosen = jnp.concatenate(
        [onehot(iota((slots, block), 0) == place) for place in places], axis=1
    )
    return dot(chosen, rows).astype(BF16)


def compact_kernel(owners, width, arrived, latent_in, routed, latent_out, sem):
    copy = pltpu.make_async_copy(latent_in, latent_out, sem)
    copy.start()
    routed[...] = compact(arrived[...], owners, width)
    copy.wait()


def on_device(
    ntm, nh, video, conv_weight, norm_gain, norm_bias, down_weight, length_table, keep, run_length, owner
):
    frames, rows, cols, chans = video.shape
    width = down_weight.shape[1]
    half_rows, half_cols = rows // 2, cols // 2
    toks = frames * half_rows * half_cols
    owners = ntm * nh
    slots = owners * CAP
    _, taken = heights(half_rows * half_cols, frames)
    ways = (4, 4) if ntm == 32 else (ntm // 2, 1)
    hbm = pl.BlockSpec(memory_space=pltpu.HBM)
    vmem = pl.BlockSpec(memory_space=pltpu.VMEM)
    tiles = CAP * width // LANES
    latent_shape = jax.ShapeDtypeStruct((frames, half_rows * half_cols, width), BF16)
    dma = pltpu.SemaphoreType.DMA
    operands = (
        video,
        conv_weight,
        norm_gain.reshape(1, chans),
        norm_bias.reshape(1, chans),
        down_weight,
        length_table,
        keep,
        run_length,
        owner,
    )
    latent, arrived = pl.pallas_call(
        functools.partial(
            encode_kernel, ntm, nh, (frames, rows, cols, chans, width), ways
        ),
        out_shape=(latent_shape, jax.ShapeDtypeStruct((owners, tiles, LANES), BF16)),
        in_specs=[hbm] * 9,
        out_specs=(vmem, vmem),
        scratch_shapes=[
            pltpu.VMEM((frames + 2, rows + 2, cols, chans), BF16),
            pltpu.VMEM((3, 3, chans, 2 * chans), BF16),
            pltpu.VMEM((3, 4, chans, 2 * chans), BF16),
            pltpu.VMEM((1, chans), F32),
            pltpu.VMEM((1, chans), F32),
            pltpu.VMEM(down_weight.shape, BF16),
            pltpu.VMEM(length_table.shape, F32),
            pltpu.VMEM(keep.shape, jnp.int32),
            pltpu.VMEM(keep.shape, jnp.int32),
            pltpu.VMEM(keep.shape, jnp.int32),
            pltpu.VMEM((frames, rows, cols, chans), F32),
            pltpu.VMEM((nh, frames, 16, chans), F32),
            pltpu.VMEM((slots, taken), BF16),
            pltpu.VMEM((taken, width), F32),
            pltpu.VMEM((taken, width), BF16),
            pltpu.VMEM((slots, width), F32),
            pltpu.VMEM((owners, tiles, LANES), BF16),
            dma((12,)),
            dma((8,)),
            dma((8,)),
            dma((frames, nh - 1)),
            dma((frames, nh)),
            pltpu.SemaphoreType.REGULAR((4,)),
            dma,
            dma,
            dma,
        ],
        compiler_params=pltpu.CompilerParams(
            collective_id=0, has_side_effects=True, vmem_limit_bytes=48 * 1024 * 1024
        ),
        name="encode",
    )(*(pltpu.with_memory_space_constraint(array, pltpu.HBM) for array in operands))
    routed, latent = pl.pallas_call(
        functools.partial(compact_kernel, owners, width),
        out_shape=(jax.ShapeDtypeStruct((slots, width), BF16), latent_shape),
        in_specs=[vmem, hbm],
        out_specs=(vmem, hbm),
        scratch_shapes=[dma],
        compiler_params=pltpu.CompilerParams(vmem_limit_bytes=48 * 1024 * 1024),
        name="compact",
    )(arrived, latent)
    return latent.reshape(frames, half_rows, half_cols, width), routed


def solution(mesh):
    return jax.shard_map(
        functools.partial(on_device, mesh.shape["tm"], mesh.shape["height"]),
        mesh=mesh,
        in_specs=(
            P("tm", "height", None, None),
            P(),
            P(),
            P(),
            P(),
            P(),
            P("tm", "height", None),
            P("tm", "height", None),
            P("tm", "height", None),
        ),
        out_specs=(P("tm", "height", None, None), P(("tm", "height"), None)),
        check_vma=False,
    )
```

time: 35 us -> 33.8 us (0.966)
  Pallas kernels: 34.3 us -> 33.1 us
    pallas_call x1, Pallas kernels: 32.5 us -> 31.3 us  [on_device(): pl.pallas_call(functools.partial(encode_kernel, ntm, nh, (frames, rows, c...]
where the time goes in v4:
time: 33.8 us; the launch traced here: 33.7 us
  Pallas kernels  33.1 us (98%)
  between operations  0.64 us (2%)
    pallas_call x1, Pallas kernels, on_device(): pl.pallas_call(functools.partial(encode_kernel, ntm, nh, (frames, rows, c...  31.3 us
    pallas_call x1, Pallas kernels, on_device(): pl.pallas_call(functools.partial(compact_kernel, owners, width), out_shap...  1.77 us

profile of v4, /device:TPU:1, one launch (start us, length us, event | category | flops | bytes accessed | tf_op | source)
XLA Modules:
  0.0 33.7 jit_solution(8035642330236660430)
XLA Ops:
  0.6 31.3 %encode.1 = (bf16[4,320,256]{2,1,0:T(8,128)(2,1)S(1)}, bf16[128,16,128]{2,1,0:T(8,128)(2,1)S(1)}) custom-call(bf16[4,8,160,128]{3,2,1,0:T(8,128)(2,1)} %video_in.1, bf16[3,3,3,128,128]{4,3,2,1,0:T(8,128)(2,1)} %weight_in.1, f32[1,128]{1,0:T(1,128)} %bitcast.3, f32[1,128]{1,0:T(1,128)} %bitcast.4, bf16[512,256]{1,0:T(8,128)(2,1)} %down_in.1, ...), custom_call_target="tpu_custom_call" | custom-call | tf_op jit(solution)/shard_map/encode/pallas_call | solution.py:502
  31.9 1.8 %compact.1 = (bf16[1024,256]{1,0:T(8,128)(2,1)}, bf16[4,320,256]{2,1,0:T(8,128)(2,1)}) custom-call(bf16[128,16,128]{2,1,0:T(8,128)(2,1)S(1)} %get-tuple-element.6.arrived, bf16[4,320,256]{2,1,0:T(8,128)(2,1)S(1)} %get-tuple-element.7.latent_in), custom_call_target="tpu_custom_call" | custom-call | tf_op jit(solution)/shard_map/compact/pallas_call | solution.py:542

commit v5 on v4

--- a/solution.py
+++ b/solution.py
@@ -13,7 +13,7 @@
 CAP = 8
 EPSILON = 1e-06
 LANES = 128
-TURNS = ((3, 2, 1, 0), (2, 3, 1, 0), (2, 3, 1, 0), (1, 0))
+TURNS = ((2, 3, 1, 0), (2, 3, 1, 0), (1, 0))
 EMPTY = 2.0**127
 LIMIT = 2.0**126
 MESH = pl.DeviceIdType.MESH
@@ -76,10 +76,19 @@
             semaphore, inc=1, device_id={"tm": t, "height": h}, device_id_type=MESH
         )
 
-    across = [
-        [(me_t, h) for h in peers],
-        [(me_t ^ (2 * k), me_h) for k in range(1, rows_x)],
-        [(me_t ^ (2 * rows_x * k), me_h) for k in range(1, planes)],
+    at_x, at_z = lax.rem(me_t // 2, rows_x), me_t // (2 * rows_x)
+    first_x = even & (at_x == 0)
+    first_z = first_x & (at_z == 0)
+    later_x, later_z = even & (at_x > 0), first_x & (at_z > 0)
+    to_first_x, to_first_z = me_t - 2 * at_x, 0
+    all_x = [me_t + 2 * k for k in range(1, rows_x)]
+    all_z = [2 * rows_x * k for k in range(1, planes)]
+    relay = [
+        (even, [(me_t, h) for h in peers], even, nh - 1),
+        (later_x, [(to_first_x, me_h)], first_x, rows_x - 1),
+        (later_z, [(to_first_z, me_h)], first_z, planes - 1),
+        (first_z, [(t, me_h) for t in all_z], later_z, 1),
+        (first_x, [(me_t + k, me_h) for k in range(1, 2 * rows_x)], jnp.logical_not(first_x), 1),
     ]
     barrier = pltpu.get_barrier_semaphore()
 
@@ -87,13 +96,18 @@
     def _():
         signal(barrier, last_t, me_h)
 
-    for t, h in across[0]:
-        signal(barrier, t, h)
-
-    @pl.when(even)
-    def _():
-        for t, h in across[1] + across[2]:
-            signal(barrier, t, h)
+    for h in peers:
+        signal(barrier, me_t, h)
+
+    @pl.when(first_x)
+    def _():
+        for t in all_x:
+            signal(barrier, t, me_h)
+
+    @pl.when(first_z)
+    def _():
+        for t in all_z:
+            signal(barrier, t, me_h)
 
     loads = [
         (keep_in, keep), (run_in, run), (owner_in, owner), (table_in, table),
@@ -112,7 +126,7 @@
     wlast[:, 3, :, pl.ds(0, chans)] = jnp.zeros((3, chans, chans), BF16)
     wlast[:, 0, :, pl.ds(chans, chans)] = jnp.zeros((3, chans, chans), BF16)
     awaited = nh - 1 + jnp.where(has_next, 1, 0)
-    pl.semaphore_wait(barrier, awaited + jnp.where(even, rows_x + planes - 2, 0))
+    pl.semaphore_wait(barrier, awaited + jnp.where(later_x | later_z, 1, 0))
 
     def halo(k, src, dst, t, h):
         return pltpu.make_async_remote_copy(
@@ -146,17 +160,19 @@
             copy.start()
 
     def tell(k):
-        @pl.when(even)
-        def _():
-            for t, h in across[k] if k < 3 else [(next_t, me_h)]:
-                signal(ready.at[k], t, h)
+        if k in (0, 4) or (rows_x, planes)[k in (2, 3)] > 1:
+
+            @pl.when(relay[k][0])
+            def _():
+                for t, h in relay[k][1]:
+                    signal(ready.at[k], t, h)
 
     def hear(k):
-        if k == 3 or across[k]:
-
-            @pl.when(even if k < 3 else jnp.logical_not(even))
+        if k in (0, 4) or (rows_x, planes)[k in (2, 3)] > 1:
+
+            @pl.when(relay[k][2])
             def _():
-                pl.semaphore_wait(ready.at[k], len(across[k]) if k < 3 else 1)
+                pl.semaphore_wait(ready.at[k], relay[k][3])
 
     tell(0)
     for copy in loads[:4]:
@@ -225,7 +241,7 @@
     def gather(lines, a, b):
         return jnp.concatenate([xbuf[t + a, r + b] for t, r in lines], axis=0)
 
-    def convolve(lines, paired, afters=(0, 1, 2)):
+    def convolve(lines, paired, afters=(0, 1, 2), more=False, sums=True):
         count = len(lines)
         window = jnp.concatenate(
             [gather(lines, a, b) for a in afters for b in range(3)], axis=1
@@ -259,13 +275,14 @@
         )
         for t in sorted({t for t, _ in lines}):
             mine = [k for k, line in enumerate(lines) if line[0] == t]
-            if afters == (0,):
-                out = out + hidden[t]
+            part = out[mine[0] : mine[-1] + 1]
+            if more:
+                part = part + hidden[t, pl.ds(lines[mine[0]][1], len(mine))]
             for k in mine:
-                hidden[t, lines[k][1]] = out[k]
-            if afters == (1, 2):
+                hidden[t, lines[k][1]] = part[k - mine[0]]
+            if not sums:
                 continue
-            tiles = out[mine[0] : mine[-1] + 1].reshape(len(mine) * cols // 8, 8, chans)
+            tiles = part.reshape(len(mine) * cols // 8, 8, chans)
             total, square = jnp.sum(tiles, axis=0), jnp.sum(tiles * tiles, axis=0)
             if not paired:
                 total = total + stat[me_h, t, pl.ds(0, 8)]
@@ -347,6 +364,8 @@
     interior, edges = range(1, rows - 1), (0, rows - 1)
     for t in range(frames - 1, 1, -1):
         convolve([(t, r) for r in interior], True)
+    convolve([(1, r) for r in interior], True, (1, 2), sums=False)
+    convolve([(0, r) for r in interior], True, (2,), sums=False)
 
     @pl.when(has_last)
     def _():
@@ -355,10 +374,10 @@
         bottom.wait_recv()
         corner_down.start()
 
+    to_up.wait_recv()
+    to_down.wait_recv()
     hear(1)
     tell(2)
-    to_up.wait_recv()
-    to_down.wait_recv()
     clear_rows(2, frames)
     convolve([(t, r) for t in range(2, frames) for r in edges], False)
     for t in range(frames - 1, 1, -1):
@@ -372,8 +391,8 @@
     def _():
         xbuf[0:2] = jnp.zeros((2, rows + 2, cols, chans), BF16)
 
-    convolve([(1, r) for r in interior], True)
-    convolve([(0, r) for r in interior], True, (1, 2))
+    convolve([(1, r) for r in interior], True, (0,), more=True)
+    convolve([(0, r) for r in interior], True, (1,), more=True, sums=False)
 
     @pl.when(has_last)
     def _():
@@ -383,40 +402,49 @@
     clear_rows(0, 2)
     convolve([(1, r) for r in edges], False)
     send_stat(1)
-    convolve([(0, r) for r in edges], False, (1, 2))
-
-    @pl.when(has_last)
-    def _():
-        early.wait_recv()
-
-    convolve([(0, r) for r in range(rows)], True, (0,))
-    send_stat(0)
+    convolve([(0, r) for r in edges], False, (1, 2), sums=False)
     hear(2)
     tell(3)
+
+    @pl.when(has_last)
+    def _():
+        early.wait_recv()
+
+    hear(3)
+    tell(4)
+    convolve([(0, r) for r in range(rows)], True, (0,), more=True)
+    send_stat(0)
     finish(range(frames - 1, 0, -1))
     rest = pl.ds(head, taken - head)
     total[...] = dot(routes[:, rest], lat[rest])
     finish([0])
-    hear(3)
+    hear(4)
     batch = owners // planes
-    turns = [[k for k in order if k < n] for order, n in zip(TURNS, (planes, rows_x, nh, 2))]
-    for z in turns[0]:
-        here = pl.ds(z * batch * CAP, batch * CAP)
+    turns = [[k for k in order if k < n] for order, n in zip(TURNS, (rows_x, nh, 2))]
+    for plane in range(planes):
+        z = at_z ^ plane
+        here = pl.ds(pl.multiple_of(z * (batch * CAP), batch * CAP), batch * CAP)
         out = dot(routes[here, pl.ds(0, head)], lat[pl.ds(0, head)]) + total[here]
         sides = [
             out[:, k * LANES : (k + 1) * LANES].reshape(batch, CAP, LANES)
             for k in range(width // LANES)
         ]
         pay[pl.ds(z * batch, batch)] = jnp.concatenate(sides, axis=1).astype(BF16)
-        for x, h, core in itertools.product(*turns[1:]):
+        for x, h, core in itertools.product(*turns):
             t = (z * rows_x + x) * 2 + core
             k = t * nh + h
-            if k:
+
+            def send():
                 pltpu.make_async_remote_copy(
                     src_ref=pay.at[k], dst_ref=arrived.at[me],
                     send_sem=go_sem, recv_sem=come_sem,
                     device_id={"tm": me_t ^ t, "height": me_h ^ h}, device_id_type=MESH,
                 ).start()
+
+            if x or h or core:
+                send()
+            else:
+                pl.when(k > 0)(send)
     mine_copy = pltpu.make_async_copy(pay.at[0], arrived.at[me], out_sem)
     mine_copy.start()
 
@@ -441,16 +469,18 @@
     pltpu.make_async_copy(pay.at[others], arrived.at[others], go_sem).wait()
 
 
-def compact(arrived, owners, width):
+def compact_kernel(owners, width, arrived, latent_in, routed, latent_out, rows, out, sem):
+    latent_copy = pltpu.make_async_copy(latent_in, latent_out, sem.at[0])
+    latent_copy.start()
     slots = owners * CAP
-    block = min(LANES, slots)
-    tall = arrived.astype(F32)
+    block, chunk = min(LANES, slots), min(2 * LANES, slots)
+    tall = arrived[...].astype(F32)
     sides = [
         tall[:, k * CAP : (k + 1) * CAP].reshape(slots, LANES) for k in range(width // LANES)
     ]
-    rows = jnp.concatenate(sides, axis=1).astype(BF16)
+    rows[...] = jnp.concatenate(sides, axis=1).astype(BF16)
     pick = onehot(iota((8, LANES), 1) == 0)
-    lead = dot_t(pick, sides[0].astype(BF16))
+    lead = dot_t(pick, rows[:, 0:LANES])
     ahead_of = onehot(iota((block, block), 0) < iota((block, block), 1))
     carry = jnp.zeros((8, 1), F32)
     places = []
@@ -459,17 +489,20 @@
         place = dot(valid.astype(BF16), ahead_of) + carry
         carry = carry + jnp.sum(valid, axis=1, keepdims=True)
         places.append(jnp.where(valid > 0.5, place, -1.0)[0:1].astype(jnp.int32))
-    chosen = jnp.concatenate(
-        [onehot(iota((slots, block), 0) == place) for place in places], axis=1
-    )
-    return dot(chosen, rows).astype(BF16)
-
-
-def compact_kernel(owners, width, arrived, latent_in, routed, latent_out, sem):
-    copy = pltpu.make_async_copy(latent_in, latent_out, sem)
-    copy.start()
-    routed[...] = compact(arrived[...], owners, width)
-    copy.wait()
+    copies = []
+    for k in range(slots // chunk):
+        at = k * chunk
+        line = iota((chunk, block), 0) + at
+        chosen = jnp.concatenate(
+            [onehot(line == place) for place in places[at // block :]], axis=1
+        )
+        out[pl.ds(at, chunk)] = dot(chosen, rows[pl.ds(at, slots - at)]).astype(BF16)
+        here = pl.ds(at, chunk)
+        copies.append(pltpu.make_async_copy(out.at[here], routed.at[here], sem.at[k + 1]))
+        copies[-1].start()
+    for copy in copies:
+        copy.wait()
+    latent_copy.wait()
 
 
 def on_device(
@@ -529,7 +562,7 @@
             dma((8,)),
             dma((frames, nh - 1)),
             dma((frames, nh)),
-            pltpu.SemaphoreType.REGULAR((4,)),
+            pltpu.SemaphoreType.REGULAR((5,)),
             dma,
             dma,
             dma,
@@ -543,8 +576,12 @@
         functools.partial(compact_kernel, owners, width),
         out_shape=(jax.ShapeDtypeStruct((slots, width), BF16), latent_shape),
         in_specs=[vmem, hbm],
-        out_specs=(vmem, hbm),
-        scratch_shapes=[dma],
+        out_specs=(hbm, hbm),
+        scratch_shapes=[
+            pltpu.VMEM((slots, width), BF16),
+            pltpu.VMEM((slots, width), BF16),
+            dma((5,)),
+        ],
         compiler_params=pltpu.CompilerParams(vmem_limit_bytes=48 * 1024 * 1024),
         name="compact",
     )(arrived, latent)

time: 33.8 us -> 32.7 us (0.967)
  Pallas kernels: 33.1 us -> 31.9 us
    pallas_call x1, Pallas kernels: 31.3 us -> 30.4 us  [on_device(): pl.pallas_call(functools.partial(encode_kernel, ntm, nh, (frames, rows, c...]
where the time goes in v5:
time: 32.7 us; the launch traced here: 32.6 us
  Pallas kernels  31.9 us (98%)
  between operations  0.64 us (2%)
    pallas_call x1, Pallas kernels, on_device(): pl.pallas_call(functools.partial(encode_kernel, ntm, nh, (frames, rows, c...  30.4 us
    pallas_call x1, Pallas kernels, on_device(): pl.pallas_call(functools.partial(compact_kernel, owners, width), out_shap...  1.53 us

profile of v5, /device:TPU:1, one launch (start us, length us, event | category | flops | bytes accessed | tf_op | source)
XLA Modules:
  0.0 32.6 jit_solution(16377471721473236999)
XLA Ops:
  0.6 30.4 %encode.1 = (bf16[4,320,256]{2,1,0:T(8,128)(2,1)S(1)}, bf16[128,16,128]{2,1,0:T(8,128)(2,1)S(1)}) custom-call(bf16[4,8,160,128]{3,2,1,0:T(8,128)(2,1)} %video_in.1, bf16[3,3,3,128,128]{4,3,2,1,0:T(8,128)(2,1)} %weight_in.1, f32[1,128]{1,0:T(1,128)} %bitcast.3, f32[1,128]{1,0:T(1,128)} %bitcast.4, bf16[512,256]{1,0:T(8,128)(2,1)} %down_in.1, ...), custom_call_target="tpu_custom_call" | custom-call | tf_op jit(solution)/shard_map/encode/pallas_call | solution.py:535
  31.1 1.5 %compact.1 = (bf16[1024,256]{1,0:T(8,128)(2,1)}, bf16[4,320,256]{2,1,0:T(8,128)(2,1)}) custom-call(bf16[128,16,128]{2,1,0:T(8,128)(2,1)S(1)} %get-tuple-element.6.arrived, bf16[4,320,256]{2,1,0:T(8,128)(2,1)S(1)} %get-tuple-element.7.latent_in), custom_call_target="tpu_custom_call" | custom-call | tf_op jit(solution)/shard_map/compact/pallas_call | solution.py:575

commit v6 on v5

--- a/solution.py
+++ b/solution.py
@@ -314,7 +314,7 @@
         )
 
     def send_stat(t):
-        for k in range(nh - 1):
+        for k in sorted(range(nh - 1), key=lambda k: -min(k + 1, nh - k - 1)):
             stat_copy(t, k).start()
 
     group_of = chans // GROUPS
@@ -410,11 +410,12 @@
     def _():
         early.wait_recv()
 
+    convolve([(0, r) for r in range(rows)], True, (0,), more=True)
+    send_stat(0)
     hear(3)
     tell(4)
-    convolve([(0, r) for r in range(rows)], True, (0,), more=True)
-    send_stat(0)
-    finish(range(frames - 1, 0, -1))
+    finish(range(frames - 1, 1, -1))
+    finish([1])
     rest = pl.ds(head, taken - head)
     total[...] = dot(routes[:, rest], lat[rest])
     finish([0])

time: 32.7 us -> 32.4 us (level)
    pallas_call x1, Pallas kernels: 30.4 us -> 30.1 us  [on_device(): pl.pallas_call(functools.partial(encode_kernel, ntm, nh, (frames, rows, c...]
where the time goes in v6:
time: 32.4 us; the launch traced here: 32.3 us
  Pallas kernels  31.6 us (98%)
  between operations  0.64 us (2%)
    pallas_call x1, Pallas kernels, on_device(): pl.pallas_call(functools.partial(encode_kernel, ntm, nh, (frames, rows, c...  30.1 us
    pallas_call x1, Pallas kernels, on_device(): pl.pallas_call(functools.partial(compact_kernel, owners, width), out_shap...  1.53 us

profile of v6, /device:TPU:1, one launch (start us, length us, event | category | flops | bytes accessed | tf_op | source)
XLA Modules:
  0.0 32.3 jit_solution(16743288879209218653)
XLA Ops:
  0.6 30.1 %encode.1 = (bf16[4,320,256]{2,1,0:T(8,128)(2,1)S(1)}, bf16[128,16,128]{2,1,0:T(8,128)(2,1)S(1)}) custom-call(bf16[4,8,160,128]{3,2,1,0:T(8,128)(2,1)} %video_in.1, bf16[3,3,3,128,128]{4,3,2,1,0:T(8,128)(2,1)} %weight_in.1, f32[1,128]{1,0:T(1,128)} %bitcast.3, f32[1,128]{1,0:T(1,128)} %bitcast.4, bf16[512,256]{1,0:T(8,128)(2,1)} %down_in.1, ...), custom_call_target="tpu_custom_call" | custom-call | tf_op jit(solution)/shard_map/encode/pallas_call | solution.py:536
  30.7 1.5 %compact.1 = (bf16[1024,256]{1,0:T(8,128)(2,1)}, bf16[4,320,256]{2,1,0:T(8,128)(2,1)}) custom-call(bf16[128,16,128]{2,1,0:T(8,128)(2,1)S(1)} %get-tuple-element.6.arrived, bf16[4,320,256]{2,1,0:T(8,128)(2,1)S(1)} %get-tuple-element.7.latent_in), custom_call_target="tpu_custom_call" | custom-call | tf_op jit(solution)/shard_map/compact/pallas_call | solution.py:576

commit v7 on v6

--- a/solution.py
+++ b/solution.py
@@ -423,7 +423,7 @@
     batch = owners // planes
     turns = [[k for k in order if k < n] for order, n in zip(TURNS, (rows_x, nh, 2))]
     for plane in range(planes):
-        z = at_z ^ plane
+        z = at_z ^ jnp.where(at_z == 0, planes - 1 - plane, plane)
         here = pl.ds(pl.multiple_of(z * (batch * CAP), batch * CAP), batch * CAP)
         out = dot(routes[here, pl.ds(0, head)], lat[pl.ds(0, head)]) + total[here]
         sides = [
@@ -472,9 +472,8 @@
 
 def compact_kernel(owners, width, arrived, latent_in, routed, latent_out, rows, out, sem):
     latent_copy = pltpu.make_async_copy(latent_in, latent_out, sem.at[0])
-    latent_copy.start()
     slots = owners * CAP
-    block, chunk = min(LANES, slots), min(2 * LANES, slots)
+    block = chunk = min(LANES, slots)
     tall = arrived[...].astype(F32)
     sides = [
         tall[:, k * CAP : (k + 1) * CAP].reshape(slots, LANES) for k in range(width // LANES)
@@ -490,6 +489,7 @@
         place = dot(valid.astype(BF16), ahead_of) + carry
         carry = carry + jnp.sum(valid, axis=1, keepdims=True)
         places.append(jnp.where(valid > 0.5, place, -1.0)[0:1].astype(jnp.int32))
+    latent_copy.start()
     copies = []
     for k in range(slots // chunk):
         at = k * chunk
@@ -581,7 +581,7 @@
         scratch_shapes=[
             pltpu.VMEM((slots, width), BF16),
             pltpu.VMEM((slots, width), BF16),
-            dma((5,)),
+            dma((9,)),
         ],
         compiler_params=pltpu.CompilerParams(vmem_limit_bytes=48 * 1024 * 1024),
         name="compact",

time: 32.4 us -> 32.3 us (level)
  no operation moved by 1% of the time
where the time goes in v7:
time: 32.3 us; the launch traced here: 32.2 us
  Pallas kernels  31.6 us (98%)
  between operations  0.64 us (2%)
    pallas_call x1, Pallas kernels, on_device(): pl.pallas_call(functools.partial(encode_kernel, ntm, nh, (frames, rows, c...  30.1 us
    pallas_call x1, Pallas kernels, on_device(): pl.pallas_call(functools.partial(compact_kernel, owners, width), out_shap...  1.5 us

profile of v7, /device:TPU:1, one launch (start us, length us, event | category | flops | bytes accessed | tf_op | source)
XLA Modules:
  0.0 32.2 jit_solution(7902178998720086384)
XLA Ops:
  0.6 30.1 %encode.1 = (bf16[4,320,256]{2,1,0:T(8,128)(2,1)S(1)}, bf16[128,16,128]{2,1,0:T(8,128)(2,1)S(1)}) custom-call(bf16[4,8,160,128]{3,2,1,0:T(8,128)(2,1)} %video_in.1, bf16[3,3,3,128,128]{4,3,2,1,0:T(8,128)(2,1)} %weight_in.1, f32[1,128]{1,0:T(1,128)} %bitcast.3, f32[1,128]{1,0:T(1,128)} %bitcast.4, bf16[512,256]{1,0:T(8,128)(2,1)} %down_in.1, ...), custom_call_target="tpu_custom_call" | custom-call | tf_op jit(solution)/shard_map/encode/pallas_call | solution.py:536
  30.7 1.5 %compact.1 = (bf16[1024,256]{1,0:T(8,128)(2,1)}, bf16[4,320,256]{2,1,0:T(8,128)(2,1)}) custom-call(bf16[128,16,128]{2,1,0:T(8,128)(2,1)S(1)} %get-tuple-element.6.arrived, bf16[4,320,256]{2,1,0:T(8,128)(2,1)S(1)} %get-tuple-element.7.latent_in), custom_call_target="tpu_custom_call" | custom-call | tf_op jit(solution)/shard_map/compact/pallas_call | solution.py:576

commit v8 on v6

--- a/solution.py
+++ b/solution.py
@@ -431,7 +431,7 @@
             for k in range(width // LANES)
         ]
         pay[pl.ds(z * batch, batch)] = jnp.concatenate(sides, axis=1).astype(BF16)
-        for x, h, core in itertools.product(*turns):
+        for core, x, h in itertools.product(turns[2], turns[0], turns[1]):
             t = (z * rows_x + x) * 2 + core
             k = t * nh + h
 
@@ -472,7 +472,6 @@
 
 def compact_kernel(owners, width, arrived, latent_in, routed, latent_out, rows, out, sem):
     latent_copy = pltpu.make_async_copy(latent_in, latent_out, sem.at[0])
-    latent_copy.start()
     slots = owners * CAP
     block, chunk = min(LANES, slots), min(2 * LANES, slots)
     tall = arrived[...].astype(F32)
@@ -490,6 +489,7 @@
         place = dot(valid.astype(BF16), ahead_of) + carry
         carry = carry + jnp.sum(valid, axis=1, keepdims=True)
         places.append(jnp.where(valid > 0.5, place, -1.0)[0:1].astype(jnp.int32))
+    latent_copy.start()
     copies = []
     for k in range(slots // chunk):
         at = k * chunk

time: 32.4 us -> 32.5 us (level)
  no operation moved by 1% of the time
where the time goes in v8:
time: 32.5 us; the launch traced here: 32.4 us
  Pallas kernels  31.7 us (98%)
  between operations  0.64 us (2%)
    pallas_call x1, Pallas kernels, on_device(): pl.pallas_call(functools.partial(encode_kernel, ntm, nh, (frames, rows, c...  30.2 us
    pallas_call x1, Pallas kernels, on_device(): pl.pallas_call(functools.partial(compact_kernel, owners, width), out_shap...  1.53 us

profile of v8, /device:TPU:1, one launch (start us, length us, event | category | flops | bytes accessed | tf_op | source)
XLA Modules:
  0.0 32.4 jit_solution(17222904012054018683)
XLA Ops:
  0.6 30.2 %encode.1 = (bf16[4,320,256]{2,1,0:T(8,128)(2,1)S(1)}, bf16[128,16,128]{2,1,0:T(8,128)(2,1)S(1)}) custom-call(bf16[4,8,160,128]{3,2,1,0:T(8,128)(2,1)} %video_in.1, bf16[3,3,3,128,128]{4,3,2,1,0:T(8,128)(2,1)} %weight_in.1, f32[1,128]{1,0:T(1,128)} %bitcast.3, f32[1,128]{1,0:T(1,128)} %bitcast.4, bf16[512,256]{1,0:T(8,128)(2,1)} %down_in.1, ...), custom_call_target="tpu_custom_call" | custom-call | tf_op jit(solution)/shard_map/encode/pallas_call | solution.py:536
  30.8 1.5 %compact.1 = (bf16[1024,256]{1,0:T(8,128)(2,1)}, bf16[4,320,256]{2,1,0:T(8,128)(2,1)}) custom-call(bf16[128,16,128]{2,1,0:T(8,128)(2,1)S(1)} %get-tuple-element.6.arrived, bf16[4,320,256]{2,1,0:T(8,128)(2,1)S(1)} %get-tuple-element.7.latent_in), custom_call_target="tpu_custom_call" | custom-call | tf_op jit(solution)/shard_map/compact/pallas_call | solution.py:576
